TPU v7x, 256 devices: a whole 4x4x8 slice. The times are simulated.
256 devices in a mesh: role: 4 (over z_hi), grp: 2 (over z_lo), tp: 32 (over x, y, core).
Axes of the slice: x: 4, y: 4, z: 8 (z_hi: 4, z_lo: 2; z = z_hi * 2 + z_lo), core: 2. Of those that a mesh axis runs over, the one named last changes fastest.
Arguments:
- x_pre: bfloat16 [4096, 7168], P(('role', 'grp'), 'tp'), may hold values from -6 to 6
- x_dec: bfloat16 [128, 7168], P(('role', 'grp'), 'tp'), may hold values from -6 to 6
- wq_a: bfloat16 [7168, 1536], P('tp'), may hold values from -0.0625 to 0.0625
- wkv_a: bfloat16 [7168, 576], P('tp'), may hold values from -0.0625 to 0.0625
- q_gain: float32 [1536], replicated, may hold values from 0.5 to 80, as said below
- kv_gain: float32 [512], replicated, may hold values from 0.25 to 1.75
- wq_b: bfloat16 [1536, 24576], P(None, 'tp'), may hold values from -0.15625 to 0.15625
- wkv_b: bfloat16 [512, 32768], P(None, 'tp'), may hold values from -0.25 to 0.25
- wo: bfloat16 [16384, 7168], P('tp'), may hold values from -0.046875 to 0.046875
- doc_len: int32 [8, 16], replicated, may hold values from 1 to 64, 512 in all within a row
- request_docs: int32 [128], replicated, may hold values from 0 to 127, each once
Outputs:
- out_pre: bfloat16 [4096, 7168], P(('role', 'grp'), 'tp')
- out_dec: bfloat16 [128, 7168], P(('role', 'grp'), 'tp')
Inputs may be any that keep to these rules, and one draw needn't show every extreme that they name: `doc_len`: row g lists the lengths of the 16 prompts packed in order into prefill group g's 512 tokens; each row sums to 512 and its longest is exactly 64. `request_docs`: prompt m is the (m % 16)-th prompt of prefill group m // 16; every prompt is continued by exactly one request. `q_gain`: positive.
All inputs are finite; a program needn't handle non-finite values.
Results may differ from a plain program's by a relative error of at most 0.03.
The roundings to bfloat16 on the way count: a program that leaves them out, or rounds other values in their place, can miss the bound.
Values may be sent and summed in bfloat16 or wider, within the bound.
A program may use at most 128 MiB of HBM per device.

v0:
```python
import jax
import jax.numpy as jnp
from jax import lax
from jax.sharding import PartitionSpec as P

KL = 512
RD = 64
NOPE = 128
VD = 128


eps = 1e-06


def rms_scale(values, gain):
    return values * lax.rsqrt(jnp.mean(values * values, axis=-1, keepdims=True) + eps) * gain


def angles(positions, width):
    half = width // 2
    freq = 10000.0 ** (-jnp.arange(half, dtype=jnp.float32) / half)
    turn = positions.astype(jnp.float32)[:, None] * freq[None, :]
    return (jnp.cos(turn), jnp.sin(turn))


def rotate(values, cosine, sine):
    half = values.shape[-1] // 2
    first = values[..., :half]
    second = values[..., half:]
    return jnp.concatenate(
        [first * cosine - second * sine, second * cosine + first * sine], axis=-1
    )


def prepare(lat_q, lat_kv, positions, q_gain, kv_gain, wq_b):
    count = lat_q.shape[0]
    latent_width = lat_kv.shape[1] - RD
    q_lat = rms_scale(lat_q, q_gain).astype(jnp.bfloat16)
    kv_c = rms_scale(lat_kv[:, :latent_width], kv_gain).astype(jnp.bfloat16)
    cosine, sine = angles(positions, RD)
    k_rope = rotate(lat_kv[:, latent_width:], cosine, sine).astype(jnp.bfloat16)
    query = jnp.dot(q_lat, wq_b, preferred_element_type=jnp.float32).reshape(count, -1, NOPE + RD)
    q_nope = query[..., :NOPE].astype(jnp.bfloat16)
    q_rope = rotate(query[..., NOPE:], cosine[:, None, :], sine[:, None, :]).astype(jnp.bfloat16)
    return (q_nope, q_rope, jnp.concatenate([kv_c, k_rope], axis=1))


def prefill_attend(q_nope, q_rope, kv_row, wkv_b, seg):
    count = kv_row.shape[0]
    kv = jnp.dot(kv_row[:, :KL], wkv_b, preferred_element_type=jnp.float32).astype(jnp.bfloat16)
    kv = kv.reshape(count, -1, NOPE + VD)
    k_nope = kv[..., :NOPE]
    values = kv[..., NOPE:]
    scale = 1.0 / float(NOPE + RD) ** 0.5
    scores = jnp.einsum("qhd,khd->hqk", q_nope, k_nope, preferred_element_type=jnp.float32)
    scores = scores + jnp.einsum(
        "qhd,kd->hqk", q_rope, kv_row[:, KL:], preferred_element_type=jnp.float32
    )
    scores = scores * scale
    rows = jnp.arange(count, dtype=jnp.int32)
    keep = (seg[:, None] == seg[None, :]) & (rows[None, :] <= rows[:, None])
    scores = jnp.where(keep[None], scores, -1e30)
    top = jnp.max(scores, axis=-1, keepdims=True)
    weights = jnp.exp(scores - top)
    probs = (weights / jnp.sum(weights, axis=-1, keepdims=True)).astype(jnp.bfloat16)
    out = jnp.einsum("hqk,khd->qhd", probs, values, preferred_element_type=jnp.float32).astype(
        jnp.bfloat16
    )
    return out.reshape(count, -1)


def decode_attend(dq_nope, dq_rope, own_row, cache, valid, wkv_b):
    count, heads = (dq_nope.shape[0], dq_nope.shape[1])
    table = wkv_b.reshape(KL, heads, NOPE + VD)
    q_abs = jnp.einsum(
        "rhd,chd->rhc", dq_nope, table[..., :NOPE], preferred_element_type=jnp.float32
    ).astype(jnp.bfloat16)
    latent = cache[..., :KL]
    rotary = cache[..., KL:]
    scale = 1.0 / float(NOPE + RD) ** 0.5
    scores = jnp.einsum("rhc,rpc->rhp", q_abs, latent, preferred_element_type=jnp.float32)
    scores = (
        scores + jnp.einsum("rhd,rpd->rhp", dq_rope, rotary, preferred_element_type=jnp.float32)
    ) * scale
    scores = jnp.where(valid[:, None, :], scores, -1e30)
    own_lat = own_row[:, :KL]
    own = jnp.einsum("rhc,rc->rh", q_abs, own_lat, preferred_element_type=jnp.float32)
    own = (
        own + jnp.einsum("rhd,rd->rh", dq_rope, own_row[:, KL:], preferred_element_type=jnp.float32)
    ) * scale
    top = jnp.maximum(jnp.max(scores, axis=-1), own)
    weights = jnp.exp(scores - top[..., None])
    own_weight = jnp.exp(own - top)
    total = jnp.sum(weights, axis=-1) + own_weight
    probs = (weights / total[..., None]).astype(jnp.bfloat16)
    own_prob = (own_weight / total).astype(jnp.bfloat16)
    lat_out = jnp.einsum("rhp,rpc->rhc", probs, latent, preferred_element_type=jnp.float32)
    lat_out = (
        lat_out + own_prob.astype(jnp.float32)[..., None] * own_lat.astype(jnp.float32)[:, None, :]
    ).astype(jnp.bfloat16)
    out = jnp.einsum(
        "rhc,chd->rhd", lat_out, table[..., NOPE:], preferred_element_type=jnp.float32
    ).astype(jnp.bfloat16)
    return out.reshape(count, -1)


def per_device(x_pre, x_dec, wq_a, wkv_a, q_gain, kv_gain, wq_b, wkv_b, wo, doc_len, request_docs):
    prompt_rows = x_pre.shape[0]
    doc_count = doc_len.shape[1]
    groups_total = doc_len.shape[0]
    longest = prompt_rows // 8
    group = lax.axis_index("role") * lax.axis_size("grp") + lax.axis_index("grp")
    part_q = jnp.dot(x_pre, wq_a, preferred_element_type=jnp.float32)
    part_kv = jnp.dot(x_pre, wkv_a, preferred_element_type=jnp.float32)
    dpart_q = jnp.dot(x_dec, wq_a, preferred_element_type=jnp.float32)
    dpart_kv = jnp.dot(x_dec, wkv_a, preferred_element_type=jnp.float32)
    lat_q, lat_kv, dlat_q, dlat_kv = lax.psum((part_q, part_kv, dpart_q, dpart_kv), "tp")
    ends_all = jnp.cumsum(doc_len, axis=1)
    starts_all = ends_all - doc_len
    lengths = lax.dynamic_slice_in_dim(doc_len, group, 1, 0)[0]
    ends = lax.dynamic_slice_in_dim(ends_all, group, 1, 0)[0]
    starts = ends - lengths
    rows = jnp.arange(prompt_rows, dtype=jnp.int32)
    seg = jnp.sum((rows[:, None] >= ends[None, :]).astype(jnp.int32), axis=1)
    onehot = (seg[:, None] == jnp.arange(doc_count, dtype=jnp.int32)[None, :]).astype(jnp.int32)
    pos = rows - jnp.sum(onehot * starts[None, :], axis=1)
    q_nope, q_rope, kv_row = prepare(lat_q, lat_kv, pos, q_gain, kv_gain, wq_b)
    docs = lax.dynamic_slice_in_dim(request_docs, group * doc_count, doc_count, 0)
    pick = (docs[:, None] == jnp.arange(groups_total * doc_count, dtype=jnp.int32)[None, :]).astype(
        jnp.int32
    )
    first_row = docs // doc_count * prompt_rows + jnp.sum(pick * starts_all.reshape(1, -1), axis=1)
    length = jnp.sum(pick * doc_len.reshape(1, -1), axis=1)
    steps = jnp.arange(longest, dtype=jnp.int32)
    index = jnp.minimum(first_row[:, None] + steps[None, :], groups_total * prompt_rows - 1)
    valid = steps[None, :] < length[:, None]
    kv_all = lax.all_gather(kv_row, ("role", "grp"), axis=0, tiled=True)
    cache = jnp.take(kv_all, index, axis=0)
    o_pre = prefill_attend(q_nope, q_rope, kv_row, wkv_b, seg)
    dq_nope, dq_rope, own_row = prepare(dlat_q, dlat_kv, length, q_gain, kv_gain, wq_b)
    o_dec = decode_attend(dq_nope, dq_rope, own_row, cache, valid, wkv_b)
    term_pre = jnp.dot(o_pre, wo, preferred_element_type=jnp.float32)
    term_dec = jnp.dot(o_dec, wo, preferred_element_type=jnp.float32)
    out_pre, out_dec = (
        lax.psum_scatter(
            term_pre.astype(jnp.bfloat16), "tp", scatter_dimension=1, tiled=True
        ).astype(jnp.float32),
        lax.psum_scatter(
            term_dec.astype(jnp.bfloat16), "tp", scatter_dimension=1, tiled=True
        ).astype(jnp.float32),
    )
    return (out_pre.astype(jnp.bfloat16), out_dec.astype(jnp.bfloat16))


def solution(mesh):
    placed = (
        P(("role", "grp"), "tp"),
        P(("role", "grp"), "tp"),
        P("tp", None),
        P("tp", None),
        P(),
        P(),
        P(None, "tp"),
        P(None, "tp"),
        P("tp", None),
        P(),
        P(),
    )
    return jax.shard_map(
        per_device,
        mesh=mesh,
        in_specs=placed,
        out_specs=(P(("role", "grp"), "tp"), P(("role", "grp"), "tp")),
        check_vma=False,
    )
```

profile of v0, /device:TPU:1, one launch (start us, length us, event | category | flops | bytes accessed | tf_op | source)
XLA Modules:
  0.0 519.1 jit_solution(14828580663528725986)
XLA Ops:
  7.3 3.7 fusion.58
  10.9 1.4 fusion.57
  12.4 0.8 fusion.59
  13.7 126.1 %all-reduce.3.cloned.1.call-done = (f32[512,1536]{1,0:T(8,128)}, f32[512,576]{0,1:T(8,128)}, f32[16,1536]{1,0:T(8,128)}) async-done(((f32[512,1536]{1,0:T(8,128)}, f32[512,576]{0,1:T(8,128)}, f32[16,1536]{1,0:T(8,128)}), (f32[512,1536]{1,0:T(8,128)}, f32[512,576]{0,1:T(8,128)}, f32[16,1536]{1,0:T(8,128)})) %all-reduce.3.cloned.1.call-update) | async-done | bytes 4423696 | tf_op jit(solution)/shard_map/psum | solution.py:117
  139.8 1.3 multiply_reduce_fusion.1
  141.2 1.4 multiply_convert_fusion.2
  142.6 1.9 subtract_convert_fusion.1
  144.4 0.9 pad_maximum_fusion
  145.4 2.3 copy.68
  147.9 0.2 select_reduce_fusion.2
  148.5 122.6 %psum.31 = f32[16,576]{1,0:T(8,128)S(1)} all-reduce(f32[16,576]{1,0:T(8,128)S(1)} %fusion.60), channel_id=1, replica_groups=mesh['role'=4,'grp'=2,'tp'=32] {'tp'}, use_global_device_ids=true, to_apply=%region_15.16 | all-reduce | flops 9216 | bytes 73728 | tf_op jit(solution)/shard_map/psum | solution.py:117
  271.1 0.7 subtract_convert_fusion.3
  271.8 0.7 maximum_bitcast_fusion.2
  272.7 0.7 iota_compare_fusion.4
  273.4 0.7 fusion.53
  274.1 0.9 fusion.13
  275.0 2.9 convolution_convert_fusion.2
  277.9 1.9 reshape.293
  279.9 1.8 fusion.32
  281.7 0.9 reshape.296
  282.6 2.3 multiply_reduce_fusion
  285.1 0.2 fusion.44
  285.3 1.2 fusion.9
  286.6 0.6 copy-done.14
  287.2 0.9 fusion.29
  288.1 2.3 fusion.4
  290.5 1.2 fusion.54
  291.6 0.7 fusion.17
  292.4 0.2 copy-done.6
  292.6 1.1 fusion.2
  293.7 1.9 copy-done.1
  295.6 0.8 fusion.55
  296.4 0.2 copy-done.8
  296.6 4.6 fusion.7
  301.3 7.7 %copy.70 = bf16[4096,576]{1,0:T(8,128)(2,1)} copy(bf16[4096,576]{0,1:T(8,128)(2,1)} %all-gather.2.cloned.1.call-done) | data formatting | bytes 9437184 | tf_op jit(solution)/shard_map/all_gather | solution.py:137
  308.9 8.5 %gather_fusion = bf16[1024,576]{1,0:T(8,128)(2,1)} fusion(bf16[4096,576]{1,0:T(8,128)(2,1)} %copy.70, s32[1024]{0:T(1024)S(1)} %broadcast_clamp_fusion), kind=kCustom, calls=%fused_computation | custom fusion | bytes 2363392 | tf_op jit(solution)/shard_map/jit(_take)/gather | solution.py:138
  317.4 1.7 broadcast_select_fusion
  319.1 0.4 fusion.15
  319.5 0.4 fusion.56
  320.1 0.3 fusion.8
  320.4 0.2 fusion.12
  320.7 4.2 convolution_convert_fusion.1
  324.9 1.7 copy.82
  326.6 0.3 reduce-scatter.5.cloned.1.call-start
  326.8 10.9 %convolution_convert_fusion = bf16[512,7168]{0,1:T(8,128)(2,1)} fusion(bf16[512,512]{0,1:T(8,128)(2,1)S(1)} %bitcast.67, bf16[512,7168]{1,0:T(8,128)(2,1)} %param.19), kind=kOutput, calls=%fused_computation.2 | convolution fusion | flops 3761766400 | bytes 15204352 | tf_op jit(solution)/shard_map/dot_general | solution.py:142
  337.8 74.8 %reduce-scatter.7.cloned.1.call-done = bf16[224,16]{1,0:T(8,128)(2,1)} async-done(((bf16[7168,16]{1,0:T(8,128)(2,1)}), bf16[224,16]{1,0:T(8,128)(2,1)}) %reduce-scatter.7.cloned.1.call-update) | async-done | bytes 7184
  412.6 1.5 copy.83
  414.1 98.4 %reduce-scatter.5.cloned.1.call-done = bf16[512,224]{0,1:T(8,128)(2,1)} async-done(((bf16[512,7168]{0,1:T(8,128)(2,1)}), bf16[512,224]{0,1:T(8,128)(2,1)}) %reduce-scatter.5.cloned.1.call-update) | async-done | bytes 229392 | tf_op jit(solution)/shard_map/reduce_scatter | solution.py:145
  (89 shorter events, 2.1 us)
Async XLA Ops:
  7.2 272.7 %copy-start = (bf16[1536,768]{1,0:T(8,128)(2,1)S(1)}, bf16[1536,768]{1,0:T(8,128)(2,1)}, u32[]{:S(2)}) copy-start(bf16[1536,768]{1,0:T(8,128)(2,1)} %param.17) | copy-start | bytes 7077892
  7.2 5.2 copy-start.3
  7.2 3.7 copy-start.5
  7.2 5.2 copy-start.18
  7.2 132.6 %all-reduce.3.cloned.1.call-start = ((), (), s32[]{:S(2)}) async-start(), calls=%async_computation.5 | async-start | bytes 8847360 | tf_op jit(solution)/shard_map/psum | solution.py:117
  7.3 3.7 copy-start.7
  10.9 2.4 copy-start.16
  12.4 128.8 %copy-start.24 = (f32[512]{0:T(512)S(1)}, f32[512]{0:T(512)}, u32[]{:S(2)}) copy-start(f32[512]{0:T(512)} %param.16) | copy-start | bytes 6148
  13.2 288.0 %all-gather.2.cloned.1.call-start = ((), (), s32[]{:S(2)}) async-start(), calls=%async_computation.3 | async-start | bytes 5308416 | tf_op jit(solution)/shard_map/all_gather | solution.py:137
  141.2 6.7 %copy-start.27 = (s32[128]{0:T(128)S(1)}, s32[128]{0:T(128)}, u32[]{:S(2)}) copy-start(s32[128]{0:T(128)} %param.21) | copy-start | bytes 1540
  144.4 3.9 copy-start.10
  145.3 267.3 %reduce-scatter.7.cloned.1.call-start = ((), (), s32[]{:S(2)}) async-start(), calls=%async_computation.4 | async-start | bytes 1892352
  147.8 132.0 %copy-start.9 = (f32[16,1536]{1,0:T(8,128)S(1)}, f32[16,1536]{1,0:T(8,128)}, u32[]{:S(2)}) copy-start(f32[16,1536]{1,0:T(8,128)} %get-tuple-element.6) | copy-start | bytes 294916
  281.7 3.3 copy-start.17
  281.7 3.4 copy-start.25
  282.6 5.4 %copy-start.2 = (f32[512,1536]{1,0:T(8,128)S(1)}, f32[512,1536]{1,0:T(8,128)}, u32[]{:S(2)}) copy-start(f32[512,1536]{1,0:T(8,128)} %get-tuple-element.4) | copy-start | bytes 9437188
  285.1 1.5 copy-start.20
  285.1 1.5 copy-start.22
  286.5 0.6 copy-start.14
  288.1 2.3 copy-start.12
  288.1 2.3 copy-start.13
  291.6 0.9 copy-start.6
  291.6 1.0 copy-start.11
  293.7 1.9 copy-start.1
  295.6 1.0 copy-start.8
  308.9 10.2 %copy-start.15 = (bf16[16,4,512]{2,0,1:T(8,128)(2,1)S(1)}, bf16[16,4,512]{2,0,1:T(8,128)(2,1)}, u32[]{:S(2)}) copy-start(bf16[16,4,512]{2,0,1:T(8,128)(2,1)} %copy-done.14) | copy-start | bytes 196612
  317.4 2.1 copy-start.21
  317.4 2.1 copy-start.23
  317.4 2.1 copy-start.26
  317.4 2.7 copy-start.19
  317.4 3.0 copy-start.4
  326.6 186.0 %reduce-scatter.5.cloned.1.call-start = ((), (), s32[]{:S(2)}) async-start(), calls=%async_computation.2 | async-start | bytes 7569408 | tf_op jit(solution)/shard_map/reduce_scatter | solution.py:145
Sparse Core Ops, SparseCore 0:
  13.4 126.4 all-reduce.2
  145.4 59.5 all-gather.1
  326.7 85.8 reduce-scatter.6
  417.1 95.3 reduce-scatter.4
where the time goes:
time: 521 us; the launch traced here: 519 us
  waiting for transfers between devices  299 us (57%)
  blocking collectives  123 us (24%)
  matrix products  38.2 us (7%)
  local copies, waits for them, and re-layouts  29 us (6%)
  other arithmetic  15.3 us (3%)
  between operations  14.1 us (3%)
    psum x1, waiting for transfers between devices, per_device(): lax.psum((part_q, part_kv, dpart_q, dpart_kv), 'tp')  126 us
    psum x1, blocking collectives, per_device(): lax.psum((part_q, part_kv, dpart_q, dpart_kv), 'tp')  123 us
    reduce_scatter x1, waiting for transfers between devices, per_device(): lax.psum_scatter(term_pre.astype(jnp.bfloat16), 'tp', scatter_dimension=1...  98.4 us
    unnamed x5, waiting for transfers between devices  74.9 us
    dot_general x1, matrix products, per_device(): term_pre = jnp.dot(o_pre, wo, preferred_element_type=jnp.float32)  10.9 us
  transfers between devices with their start and end apart: 4, of which 3 were waited for; matrix products, arithmetic and copies ran while one was open for 8% of the time, Pallas kernels for 0%

commit v1 on v0

v1 whole, which is shorter than its diff:
```python
import functools

import jax
import jax.numpy as jnp
from jax import lax
from jax.experimental import pallas as pl
from jax.experimental.pallas import tpu as pltpu
from jax.sharding import PartitionSpec as P

QL = 1536
KL = 512
RD = 64
NOPE = 128
VD = 128
NX = 4
NY = 4
W = QL + KL + 128
SPLIT = 1152
EPS = 1e-06
F32 = jnp.float32
BF16 = jnp.bfloat16
MESH = pl.DeviceIdType.MESH
VMEM_LIMIT = 58 * 2**20


def place():
    tp = lax.axis_index("tp")
    return tp, tp // 8, lax.rem(tp // 2, NY), lax.rem(tp, 2)


def tp_of(x, y, c):
    return x * 8 + y * 2 + c


def next_of(p, step):
    return lax.rem(p + step + 4, 4)


def z_peer(step):
    z = lax.axis_index("role") * 2 + lax.axis_index("grp")
    other = lax.rem(z + step, 8)
    return z, other, {"role": other // 2, "grp": lax.rem(other, 2)}


def remote(src, dst, send, recv, device):
    return pltpu.make_async_remote_copy(
        src_ref=src, dst_ref=dst, send_sem=send, recv_sem=recv, device_id=device, device_id_type=MESH
    )


def chip_peer(x, y, c, step):
    other = lax.rem(x * 4 + y + step, 16)
    return other, {"tp": tp_of(other // 4, lax.rem(other, 4), c)}


def greet(x, y, c):
    barrier = pltpu.get_barrier_semaphore()
    pl.semaphore_signal(barrier, inc=1, device_id={"tp": tp_of(x, y, 1 - c)}, device_id_type=MESH)

    def chips(step, carry):
        _, device = chip_peer(x, y, c, step)
        pl.semaphore_signal(barrier, inc=1, device_id=device, device_id_type=MESH)
        return carry

    lax.fori_loop(1, 16, chips, 0)

    def planes(step, carry):
        _, _, device = z_peer(step)
        pl.semaphore_signal(barrier, inc=1, device_id=device, device_id_type=MESH)
        return carry

    lax.fori_loop(1, 8, planes, 0)
    pl.semaphore_wait(barrier, 1 + 15 + 7)


class Ring:
    def __init__(self, data, near, far, part, pos, plus, minus, send, recv, base):
        self.data, self.near, self.far, self.part = data, near, far, part
        self.pos, self.plus, self.minus = pos, plus, minus
        self.send, self.recv, self.base = send, recv, base
        self.copies = {}

    def cut(self, ref, side):
        return ref.at[(Ellipsis, self.part[side])]

    def go(self, key, number, src, dst, device):
        copy = remote(src, dst, self.send.at[self.base + number], self.recv.at[self.base + number], device)
        copy.start()
        self.copies[key] = copy

    def start_far(self):
        chunk = self.data.at[next_of(self.pos, 2)]
        self.go("far0", 0, self.cut(chunk, 0), self.cut(self.far, 0), self.plus)
        self.go("far1", 1, self.cut(chunk, 1), self.cut(self.far, 1), self.minus)

    def start_near(self):
        up, down = self.data.at[next_of(self.pos, 1)], self.data.at[next_of(self.pos, -1)]
        self.go("up1", 2, self.cut(up, 1), self.cut(self.near.at[0], 1), self.plus)
        self.go("down0", 3, self.cut(down, 0), self.cut(self.near.at[1], 0), self.minus)

    def add(self, chunk, side):
        ref, extra = self.cut(chunk, side), self.cut(self.far, side)
        ref[...] = (ref[...].astype(F32) + extra[...].astype(F32)).astype(ref.dtype)

    def pass_on(self):
        up, down = self.data.at[next_of(self.pos, 1)], self.data.at[next_of(self.pos, -1)]
        self.copies["far0"].wait_recv()
        self.add(up, 0)
        self.go("up0", 4, self.cut(up, 0), self.cut(self.near.at[0], 0), self.plus)
        self.copies["far1"].wait_recv()
        self.add(down, 1)
        self.go("down1", 5, self.cut(down, 1), self.cut(self.near.at[1], 1), self.minus)

    def result(self, side):
        for key in ("up%d" % side, "down%d" % side):
            self.copies[key].wait_recv()
        own = self.cut(self.data.at[self.pos], side)[...].astype(F32)
        left = self.cut(self.near.at[0], side)[...].astype(F32)
        right = self.cut(self.near.at[1], side)[...].astype(F32)
        return own + (left + right)

    def close(self):
        for copy in self.copies.values():
            copy.wait_send()


def latent_rows(rows, q_gain, kv_gain, cosine, sine):
    q = rows[:, :QL]
    kv = rows[:, QL : QL + KL]
    turn = rows[:, QL + KL :]
    q = q * lax.rsqrt(jnp.mean(q * q, axis=-1, keepdims=True) + EPS) * q_gain
    kv = kv * lax.rsqrt(jnp.mean(kv * kv, axis=-1, keepdims=True) + EPS) * kv_gain
    turn = rope_tile(turn, cosine, sine)
    lane = lax.broadcasted_iota(jnp.int32, turn.shape, 1)
    turn = jnp.where(lane < RD, turn, 0.0)
    return q, kv, turn


def rope_tile(tile, cosine, sine):
    lane = lax.broadcasted_iota(jnp.int32, tile.shape, 1)
    swapped = jnp.where(lane % RD < RD // 2, pltpu.roll(tile, 96, 1), pltpu.roll(tile, 32, 1))
    return tile * cosine + swapped * sine


def down_kernel(
    xt_ref, xd_ref, wqa_ref, wkva_ref, sel_ref, qg_ref, kvg_ref, cos_ref, sin_ref, cosd_ref, sind_ref,
    out_ref, outd_ref,
    wkv_s, p0, p1, c0, c1, near0, near1, far0, far1, q0, q1, qnear0, qnear1, qfar0, qfar1,
    xd_all, dec, dec_in, tiles, tiles_in, sums_in, rows_in,
    zs, zr, cs, cr, rs, rr, ds, dr, es, er, gs, gr, ks, kr, ms, mr,
):
    tp, x, y, c = place()
    peer = {"tp": tp_of(x, y, 1 - c)}
    xp, xm = {"tp": tp_of(next_of(x, 1), y, c)}, {"tp": tp_of(next_of(x, -1), y, c)}
    yp, ym = {"tp": tp_of(x, next_of(y, 1), c)}, {"tp": tp_of(x, next_of(y, -1), c)}
    greet(x, y, c)

    z, _, _ = z_peer(0)
    xd_all[z] = xd_ref[...]

    def send_z(step, carry):
        zz, _, device = z_peer(step)
        remote(xd_ref, xd_all.at[zz], zs.at[step], zr.at[step], device).start()
        return carry

    lax.fori_loop(1, 8, send_z, 0)

    wkv_s[...] = jnp.zeros_like(wkv_s)
    wkv_s[:, : KL + RD] = wkva_ref[...]

    dims = (((0,), (0,)), ((), ()))
    order = (2, 1, 3, 0)
    core0, core1 = [], []
    for i, d in enumerate(order):
        xx = next_of(x, d)
        rows = xt_ref[:, pl.ds(pl.multiple_of(xx * 128, 128), 128)]
        for w_ref, lo, wide in ((wqa_ref, 0, QL), (wkv_s, QL, W - QL)):
            val = lax.dot_general(rows, w_ref[...], dims, preferred_element_type=F32)
            val = val.reshape(NY, 2, 2, 8, wide)
            for cc in range(2):
                p0[cc, xx, :, :, lo : lo + wide] = val[:, cc, 0]
                for yy in range(NY):
                    p1[cc, yy, xx, :, lo : lo + wide] = val[yy, cc, 1]
        copy = remote(p0.at[1 - c, xx], c0.at[xx], cs.at[i], cr.at[i], peer)
        copy.start()
        core0.append(copy)
    for i, d in enumerate(order):
        yy = next_of(y, d)
        copy = remote(p1.at[1 - c, yy], c1.at[yy], cs.at[4 + i], cr.at[4 + i], peer)
        copy.start()
        core1.append(copy)

    own0, own1 = p0.at[c], p1.at[c]
    lanes = (slice(0, SPLIT), slice(SPLIT, W))
    ring0 = Ring(own0, near0, far0, lanes, x, xp, xm, rs, rr, 0)
    ring1 = Ring(own1, near1, far1, lanes, y, yp, ym, rs, rr, 6)
    both = ((ring0, own0, c0, core0, x), (ring1, own1, c1, core1, y))

    def take_core(i):
        for ring, own, came, copies, pos in both:
            copies[i].wait_recv()
            k = next_of(pos, order[i])
            own[k] = own[k] + came[k]

    take_core(0)
    ring0.start_far()
    ring1.start_far()
    take_core(1)
    take_core(2)
    ring0.start_near()
    ring1.start_near()
    take_core(3)

    def wait_z(step, carry):
        zz, other, device = z_peer(step)
        remote(xd_ref, xd_all.at[zz], zs.at[step], zr.at[step], device).wait()
        return carry

    lax.fori_loop(1, 8, wait_z, 0)
    asked = jnp.dot(sel_ref[...], xd_all[...].reshape(128, -1), preferred_element_type=F32).astype(BF16)
    for w_ref, lo, wide in ((wqa_ref, 0, QL), (wkv_s, QL, W - QL)):
        val = jnp.dot(asked, w_ref[...], preferred_element_type=F32)
        dec[:, :, lo : lo + wide] = val.reshape(2, 8, wide)
    dec_core = remote(dec.at[1 - c], dec_in, ds.at[0], dr.at[0], peer)
    dec_core.start()

    ring0.pass_on()
    ring1.pass_on()

    dec_core.wait()
    mine = dec[c] + dec_in[...]
    chip = x * 4 + y
    for j in range(16):
        tiles[j, :, 0:128] = mine[:, 128 * j : 128 * j + 128]
        tiles[j, :, 128:256] = mine[:, QL + KL :]

    def send_tile(step, carry):
        other, device = chip_peer(x, y, c, step)
        remote(tiles.at[other], tiles_in.at[chip], es.at[step], er.at[step], device).start()
        return carry

    lax.fori_loop(1, 16, send_tile, 0)
    tiles_in[chip] = tiles[chip]

    for side in range(2):
        q0[:, :, lanes[side]] = ring0.result(side)
        q1[:, :, lanes[side]] = ring1.result(side)
    last0 = Ring(q0, qnear0, qfar0, lanes, y, yp, ym, rs, rr, 12)
    last1 = Ring(q1, qnear1, qfar1, lanes, x, xp, xm, rs, rr, 18)
    for ring in (last0, last1):
        ring.start_far()
        ring.start_near()

    def wait_tile(step, carry):
        other, device = chip_peer(x, y, c, step)
        remote(tiles.at[other], tiles_in.at[chip], es.at[step], er.at[step], device).wait()
        return carry

    lax.fori_loop(1, 16, wait_tile, 0)
    total = jnp.sum(tiles_in[...], axis=0)
    sums_in[chip] = total[:, :128]

    def send_sum(step, carry):
        other, device = chip_peer(x, y, c, step)
        remote(sums_in.at[chip], sums_in.at[chip], gs.at[step], gr.at[step], device).start()
        return carry

    lax.fori_loop(1, 16, send_sum, 0)

    last0.pass_on()
    last1.pass_on()

    parts = [[ring.result(side) for side in range(2)] for ring in (last0, last1)]
    rows = jnp.concatenate([jnp.concatenate(part, axis=1) for part in parts], axis=0)
    q, kv, turn = latent_rows(rows, qg_ref[...], kvg_ref[...], cos_ref[tp], sin_ref[tp])
    out_ref[x, y, c, :, 0:QL] = q.astype(BF16)
    out_ref[x, y, c, :, QL : QL + KL] = kv.astype(BF16)
    out_ref[x, y, c, :, QL + KL : W] = turn.astype(BF16)

    copies = []
    ka, kb = slice(0, SPLIT), slice(SPLIT, W)
    cuts = ((slice(0, 640), slice(640, SPLIT)), (slice(SPLIT, 1664), slice(1664, W)))
    count = [0]

    def push(block, device):
        n = count[0]
        count[0] += 1
        copy = remote(block, block, ks.at[n], kr.at[n], device)
        copy.start()
        copies.append(copy)
        return copy

    mate = lambda xs, ys, cols: push(out_ref.at[xs, ys, c, :, cols], peer)
    xl, xr, yl, yr = next_of(x, -1), next_of(x, 1), next_of(y, -1), next_of(y, 1)
    a_right = push(out_ref.at[x, y, c, :, ka], xp)
    a_left = push(out_ref.at[x, y, c, :, ka], xm)
    b_right = push(out_ref.at[x, y, c, :, kb], yp)
    b_left = push(out_ref.at[x, y, c, :, kb], ym)
    a_right.wait_recv()
    f1 = push(out_ref.at[xl, y, c, :, cuts[0][0]], xp)
    a_left.wait_recv()
    f2 = push(out_ref.at[xr, y, c, :, cuts[0][1]], xm)
    b_right.wait_recv()
    f3 = push(out_ref.at[x, yl, c, :, cuts[1][0]], yp)
    b_left.wait_recv()
    f4 = push(out_ref.at[x, yr, c, :, cuts[1][1]], ym)

    def wait_sum(step, carry):
        other, device = chip_peer(x, y, c, step)
        remote(sums_in.at[chip], sums_in.at[chip], gs.at[step], gr.at[step], device).wait()
        return carry

    lax.fori_loop(1, 16, wait_sum, 0)
    for j in range(16):
        rows_in[c, :, 128 * j : 128 * j + 128] = sums_in[j]
    rows_in[c, :, QL + KL : W] = total[:, 128:]
    dec_mate = remote(rows_in.at[c], rows_in.at[c], ms.at[0], mr.at[0], peer)
    dec_mate.start()

    f1.wait_recv()
    f2.wait_recv()
    f3.wait_recv()
    f4.wait_recv()
    every = slice(None)
    a2_right = push(out_ref.at[:, y, c, :, ka], yp)
    a2_left = push(out_ref.at[:, y, c, :, ka], ym)
    b2_right = push(out_ref.at[x, :, c, :, kb], xp)
    b2_left = push(out_ref.at[x, :, c, :, kb], xm)
    mates = [mate(every, y, ka), mate(x, every, kb)]
    dec_mate.wait()
    q, kv, turn = latent_rows(rows_in[...].reshape(16, W), qg_ref[...], kvg_ref[...], cosd_ref[...], sind_ref[...])
    outd_ref[:, 0:QL] = q.astype(BF16)
    outd_ref[:, QL : QL + KL] = kv.astype(BF16)
    outd_ref[:, QL + KL : W] = turn.astype(BF16)
    a2_right.wait_recv()
    g1 = push(out_ref.at[:, yl, c, :, cuts[0][0]], yp)
    a2_left.wait_recv()
    g2 = push(out_ref.at[:, yr, c, :, cuts[0][1]], ym)
    b2_right.wait_recv()
    g3 = push(out_ref.at[xl, :, c, :, cuts[1][0]], xp)
    b2_left.wait_recv()
    g4 = push(out_ref.at[xr, :, c, :, cuts[1][1]], xm)
    mates += [mate(every, yl, ka), mate(every, yr, ka), mate(xl, every, kb), mate(xr, every, kb)]
    g1.wait_recv()
    g2.wait_recv()
    mates.append(mate(every, next_of(y, 2), ka))
    g3.wait_recv()
    g4.wait_recv()
    mates.append(mate(next_of(x, 2), every, kb))
    for copy in mates:
        copy.wait_recv()
    for copy in copies:
        copy.wait_send()
    for copy in core0 + core1:
        copy.wait_send()
    for ring in (ring0, ring1, last0, last1):
        ring.close()


def down(xt, xd, wq_a, wkv_a, sel, q_gain, kv_gain, cosine, sine, cosd, sind):
    vm = pl.BlockSpec(memory_space=pltpu.VMEM)
    dma = pltpu.SemaphoreType.DMA
    return pl.pallas_call(
        down_kernel,
        out_shape=(
            jax.ShapeDtypeStruct((NX, NY, 2, 16, W), BF16),
            jax.ShapeDtypeStruct((16, W), BF16),
        ),
        in_specs=[vm] * 11,
        out_specs=(vm, vm),
        scratch_shapes=[
            pltpu.VMEM((wq_a.shape[0], W - QL), BF16),
            pltpu.VMEM((2, 4, 4, 8, W), F32),
            pltpu.VMEM((2, 4, 4, 8, W), F32),
            pltpu.VMEM((4, 4, 8, W), F32),
            pltpu.VMEM((4, 4, 8, W), F32),
            pltpu.VMEM((2, 4, 8, W), F32),
            pltpu.VMEM((2, 4, 8, W), F32),
            pltpu.VMEM((4, 8, W), F32),
            pltpu.VMEM((4, 8, W), F32),
            pltpu.VMEM((4, 8, W), F32),
            pltpu.VMEM((4, 8, W), F32),
            pltpu.VMEM((2, 8, W), F32),
            pltpu.VMEM((2, 8, W), F32),
            pltpu.VMEM((8, W), F32),
            pltpu.VMEM((8, W), F32),
            pltpu.VMEM((8,) + xd.shape, BF16),
            pltpu.VMEM((2, 8, W), F32),
            pltpu.VMEM((8, W), F32),
            pltpu.VMEM((16, 8, 256), F32),
            pltpu.VMEM((16, 8, 256), F32),
            pltpu.VMEM((16, 8, 128), F32),
            pltpu.VMEM((2, 8, W), F32),
        ]
        + [dma((n,)) for n in (8, 8, 8, 8, 24, 24, 1, 1, 16, 16, 16, 16, 24, 24, 1, 1)],
        compiler_params=pltpu.CompilerParams(
            collective_id=0, has_side_effects=True, vmem_limit_bytes=VMEM_LIMIT
        ),
        name="down",
    )(xt, xd, wq_a, wkv_a, sel, q_gain, kv_gain, cosine, sine, cosd, sind)


NT = (((1,), (1,)), ((), ()))


def split_query(query, cosine, sine):
    nope, rope = [], []
    lane = lax.broadcasted_iota(jnp.int32, (query.shape[0], 128), 1)
    for pair in range(query.shape[1] // 384):
        t0, t1, t2 = [query[:, 384 * pair + 128 * i : 384 * pair + 128 * i + 128] for i in range(3)]
        nope.append(t0.astype(BF16))
        nope.append(jnp.where(lane < 64, pltpu.roll(t1, 64, 1), pltpu.roll(t2, 64, 1)).astype(BF16))
        rope.append(rope_tile(jnp.where(lane < 64, t1, t2), cosine, sine).astype(BF16))
    return nope, rope


def attend_kernel(
    z_ref, zd_ref, wqb_ref, wkvb_ref, cos_ref, sin_ref, cosd_ref, sind_ref, segc_ref, segr_ref,
    o_ref, od_ref, kv_s,
):
    count = z_ref.shape[0]
    heads = wqb_ref.shape[1] // (NOPE + RD)
    scale = 1.0 / float(NOPE + RD) ** 0.5
    wide = NOPE + VD

    def project(i, carry):
        rows = pl.ds(pl.multiple_of(i * 128, 128), 128)
        kv = jnp.dot(z_ref[rows, QL : QL + KL], wkvb_ref[...], preferred_element_type=F32)
        kv_s[rows, :] = kv.astype(BF16)
        return carry

    lax.fori_loop(0, count // 128, project, 0)

    def block(i, carry):
        first = pl.multiple_of(i * 128, 128)
        begin = pl.multiple_of(jnp.maximum(i - 1, 0) * 128, 128)
        rows, keys = pl.ds(first, 128), pl.ds(begin, 256)
        query = jnp.dot(z_ref[rows, :QL], wqb_ref[...], preferred_element_type=F32)
        nope, rope = split_query(query, cos_ref[rows, :], sin_ref[rows, :])
        turn = z_ref[keys, QL + KL : W].astype(F32)
        turns = (turn.astype(BF16), pltpu.roll(turn, 64, 1).astype(BF16))
        own = first + lax.broadcasted_iota(jnp.int32, (128, 256), 0)
        other = begin + lax.broadcasted_iota(jnp.int32, (128, 256), 1)
        keep = (segc_ref[rows, 0:1] == segr_ref[0:1, keys]) & (other <= own)
        for h in range(heads):
            q = jnp.concatenate([nope[h], rope[h // 2]], axis=1)
            k = jnp.concatenate([kv_s[keys, wide * h : wide * h + NOPE], turns[h % 2]], axis=1)
            s = lax.dot_general(q, k, NT, preferred_element_type=F32) * scale
            s = jnp.where(keep, s, -1e30)
            e = jnp.exp(s - jnp.max(s, axis=-1, keepdims=True))
            p = (e / jnp.sum(e, axis=-1, keepdims=True)).astype(BF16)
            v = kv_s[keys, wide * h + NOPE : wide * h + wide]
            o = jnp.dot(p, v, preferred_element_type=F32)
            o_ref[rows, VD * h : VD * h + VD] = o.astype(BF16)
        return carry

    lax.fori_loop(0, count // 128, block, 0)

    query = jnp.dot(zd_ref[:, :QL], wqb_ref[...], preferred_element_type=F32)
    nope, rope = split_query(query, cosd_ref[...], sind_ref[...])
    latent, own_lat = z_ref[:, QL : QL + KL], zd_ref[:, QL : QL + KL]
    turn, own_turn = z_ref[:, QL + KL : W].astype(F32), zd_ref[:, QL + KL : W].astype(F32)
    turns = (turn.astype(BF16), pltpu.roll(turn, 64, 1).astype(BF16))
    own_turns = (own_turn.astype(BF16), pltpu.roll(own_turn, 64, 1).astype(BF16))
    doc = lax.broadcasted_iota(jnp.int32, (16, count), 0)
    keep = doc == segr_ref[0:1, :]
    diag = lax.broadcasted_iota(jnp.int32, (16, 16), 0) == lax.broadcasted_iota(jnp.int32, (16, 16), 1)
    for h in range(heads):
        up = wkvb_ref[:, wide * h : wide * h + NOPE]
        q_abs = lax.dot_general(nope[h], up, NT, preferred_element_type=F32).astype(BF16)
        s = lax.dot_general(q_abs, latent, NT, preferred_element_type=F32)
        s = (s + lax.dot_general(rope[h // 2], turns[h % 2], NT, preferred_element_type=F32)) * scale
        s = jnp.where(keep, s, -1e30)
        t = lax.dot_general(q_abs, own_lat, NT, preferred_element_type=F32)
        t = (t + lax.dot_general(rope[h // 2], own_turns[h % 2], NT, preferred_element_type=F32)) * scale
        t = jnp.where(diag, t, -1e30)
        top = jnp.maximum(jnp.max(s, axis=-1, keepdims=True), jnp.max(t, axis=-1, keepdims=True))
        e, f = jnp.exp(s - top), jnp.exp(t - top)
        total = jnp.sum(e, axis=-1, keepdims=True) + jnp.sum(f, axis=-1, keepdims=True)
        lat = jnp.dot((e / total).astype(BF16), latent, preferred_element_type=F32)
        lat = lat + jnp.dot((f / total).astype(BF16), own_lat, preferred_element_type=F32)
        down_v = wkvb_ref[:, wide * h + NOPE : wide * h + wide]
        o = jnp.dot(lat.astype(BF16), down_v, preferred_element_type=F32)
        od_ref[:, VD * h : VD * h + VD] = o.astype(BF16)


def attend(z, zd, wq_b, wkv_b, cosine, sine, cosd, sind, segc, segr):
    vm = pl.BlockSpec(memory_space=pltpu.VMEM)
    return pl.pallas_call(
        attend_kernel,
        out_shape=(
            jax.ShapeDtypeStruct((z.shape[0], 512), BF16),
            jax.ShapeDtypeStruct((16, 512), BF16),
        ),
        in_specs=[vm] * 10,
        out_specs=(vm, vm),
        scratch_shapes=[pltpu.VMEM((z.shape[0], wkv_b.shape[1]), BF16)],
        compiler_params=pltpu.CompilerParams(vmem_limit_bytes=VMEM_LIMIT),
        name="attend",
    )(z, zd, wq_b, wkv_b, cosine, sine, cosd, sind, segc, segr)


def up_kernel(
    o_ref, od_ref, wo_ref, sel_ref, out_ref, outd_ref,
    t0, t1, c0, c1, near0, near1, far0, far1, q0, q1, qnear0, qnear1, qfar0, qfar1,
    dd, dt, dc, dn, dz,
    cs, cr, rs, rr, ds, dr, es, er, zs, zr,
):
    tp, x, y, c = place()
    cols = 224
    peer = {"tp": tp_of(x, y, 1 - c)}
    xp, xm = {"tp": tp_of(next_of(x, 1), y, c)}, {"tp": tp_of(next_of(x, -1), y, c)}
    yp, ym = {"tp": tp_of(x, next_of(y, 1), c)}, {"tp": tp_of(x, next_of(y, -1), c)}
    greet(x, y, c)

    dims = (((0,), (1,)), ((), ()))
    dd[...] = jnp.zeros_like(dd)

    def part(k, carry):
        w = wo_ref[:, pl.ds(pl.multiple_of(k * 896, 128), 896)]
        xx, yy = k // 2, 2 * lax.rem(k, 2)
        dd[:, :896] = jnp.dot(od_ref[...], w, preferred_element_type=F32)
        for j in range(4):
            at = 224 * j // 128 * 128
            v = dd[:, at : at + 384]
            if 224 * j - at:
                v = pltpu.roll(v, 384 - (224 * j - at), 1)
            dt[j % 2, 2 * k + j // 2] = v[:, :256].astype(BF16)
        val = lax.dot_general(w, o_ref[...], dims, preferred_element_type=F32).astype(BF16)
        for j in range(4):
            blk = val[224 * j : 224 * j + 224]
            t0[j % 2, xx, yy + j // 2] = blk[:, :256]
            t1[j % 2, yy + j // 2, xx] = blk[:, 256:]
        return carry

    lax.fori_loop(0, 8, part, 0)

    dec_core = remote(dt.at[1 - c], dc, ds.at[0], dr.at[0], peer)
    dec_core.start()
    order = (2, 1, 3, 0)
    core0, core1 = [], []
    for i, d in enumerate(order):
        for n, (t, came, pos, copies) in enumerate(((t0, c0, x, core0), (t1, c1, y, core1))):
            k = next_of(pos, d)
            copy = remote(t.at[1 - c, k], came.at[k], cs.at[2 * i + n], cr.at[2 * i + n], peer)
            copy.start()
            copies.append(copy)
    own0, own1 = t0.at[c], t1.at[c]
    lanes = (slice(0, 128), slice(128, 256))
    ring0 = Ring(own0, near0, far0, lanes, x, xp, xm, rs, rr, 0)
    ring1 = Ring(own1, near1, far1, lanes, y, yp, ym, rs, rr, 6)
    both = ((ring0, own0, c0, core0, x), (ring1, own1, c1, core1, y))

    dec_core.wait()
    chip = x * 4 + y
    dt[c] = (dt[c].astype(F32) + dc[...].astype(F32)).astype(BF16)

    def send_tile(step, carry):
        other, device = chip_peer(x, y, c, step)
        remote(dt.at[c, other], dn.at[chip], es.at[step], er.at[step], device).start()
        return carry

    lax.fori_loop(1, 16, send_tile, 0)
    dn[chip] = dt[c, chip]

    def take_core(i):
        for ring, own, came, copies, pos in both:
            copies[i].wait_recv()
            k = next_of(pos, order[i])
            own[k] = (own[k].astype(F32) + came[k].astype(F32)).astype(BF16)

    take_core(0)
    ring0.start_far()
    ring1.start_far()
    take_core(1)
    take_core(2)
    ring0.start_near()
    ring1.start_near()
    take_core(3)

    def wait_tile(step, carry):
        other, device = chip_peer(x, y, c, step)
        remote(dt.at[c, other], dn.at[chip], es.at[step], er.at[step], device).wait()
        return carry

    lax.fori_loop(1, 16, wait_tile, 0)
    z, _, _ = z_peer(0)
    dz[z] = jnp.sum(dn[...].astype(F32), axis=0).astype(BF16)

    def send_z(step, carry):
        zz, _, device = z_peer(step)
        remote(dz.at[zz], dz.at[zz], zs.at[step], zr.at[step], device).start()
        return carry

    lax.fori_loop(1, 8, send_z, 0)

    ring0.pass_on()
    ring1.pass_on()
    for side in range(2):
        q0[:, :, lanes[side]] = ring0.result(side).astype(BF16)
        q1[:, :, lanes[side]] = ring1.result(side).astype(BF16)
    last0 = Ring(q0, qnear0, qfar0, lanes, y, yp, ym, rs, rr, 12)
    last1 = Ring(q1, qnear1, qfar1, lanes, x, xp, xm, rs, rr, 18)
    for ring in (last0, last1):
        ring.start_far()
        ring.start_near()

    def wait_z(step, carry):
        zz, _, device = z_peer(step)
        remote(dz.at[zz], dz.at[zz], zs.at[step], zr.at[step], device).wait()
        return carry

    lax.fori_loop(1, 8, wait_z, 0)
    asked = jnp.dot(sel_ref[...], dz[...].reshape(128, 256), preferred_element_type=F32)
    outd_ref[...] = asked[:, :cols].astype(BF16)

    last0.pass_on()
    last1.pass_on()
    for h, ring in enumerate((last0, last1)):
        for side in range(2):
            at = 256 * h + 128 * side
            out_ref[:, at : at + 128] = ring.result(side).astype(BF16)
    for copy in core0 + core1:
        copy.wait_send()
    for ring in (ring0, ring1, last0, last1):
        ring.close()


def up(o, od, wo, sel):
    vm = pl.BlockSpec(memory_space=pltpu.VMEM)
    dma = pltpu.SemaphoreType.DMA
    return pl.pallas_call(
        up_kernel,
        out_shape=(
            jax.ShapeDtypeStruct((224, 512), BF16),
            jax.ShapeDtypeStruct((16, 224), BF16),
        ),
        in_specs=[vm] * 4,
        out_specs=(vm, vm),
        scratch_shapes=[
            pltpu.VMEM((2, 4, 4, 224, 256), BF16),
            pltpu.VMEM((2, 4, 4, 224, 256), BF16),
            pltpu.VMEM((4, 4, 224, 256), BF16),
            pltpu.VMEM((4, 4, 224, 256), BF16),
            pltpu.VMEM((2, 4, 224, 256), BF16),
            pltpu.VMEM((2, 4, 224, 256), BF16),
            pltpu.VMEM((4, 224, 256), BF16),
            pltpu.VMEM((4, 224, 256), BF16),
            pltpu.VMEM((4, 224, 256), BF16),
            pltpu.VMEM((4, 224, 256), BF16),
            pltpu.VMEM((2, 224, 256), BF16),
            pltpu.VMEM((2, 224, 256), BF16),
            pltpu.VMEM((224, 256), BF16),
            pltpu.VMEM((224, 256), BF16),
            pltpu.VMEM((16, 1024), F32),
            pltpu.VMEM((2, 16, 16, 256), BF16),
            pltpu.VMEM((16, 16, 256), BF16),
            pltpu.VMEM((16, 16, 256), BF16),
            pltpu.VMEM((8, 16, 256), BF16),
        ]
        + [dma((n,)) for n in (8, 8, 24, 24, 1, 1, 16, 16, 8, 8)],
        compiler_params=pltpu.CompilerParams(
            collective_id=1, has_side_effects=True, vmem_limit_bytes=VMEM_LIMIT
        ),
        name="up",
    )(o, od, wo, sel)


def tables(positions):
    half = RD // 2
    freq = 10000.0 ** (-jnp.arange(half, dtype=F32) / half)
    turn = positions.astype(F32)[:, None] * freq[None, :]
    cosine, sine = jnp.cos(turn), jnp.sin(turn)
    return jnp.tile(cosine, (1, 4)), jnp.tile(jnp.concatenate([-sine, sine], axis=1), (1, 2))


def per_device(x_pre, x_dec, wq_a, wkv_a, q_gain, kv_gain, wq_b, wkv_b, wo, doc_len, request_docs):
    count = x_pre.shape[0]
    docs = doc_len.shape[1]
    group = lax.axis_index("role") * lax.axis_size("grp") + lax.axis_index("grp")
    lengths = lax.dynamic_slice_in_dim(doc_len, group, 1, 0)[0]
    ends = jnp.cumsum(lengths)
    starts = ends - lengths
    rows = jnp.arange(count, dtype=jnp.int32)
    past = rows[:, None] >= ends[None, :]
    seg = jnp.sum(past.astype(jnp.int32), axis=1)
    pos = rows - jnp.sum(jnp.where(past, lengths[None, :], 0), axis=1)
    cosine, sine = tables(jnp.concatenate([pos, lengths]))
    cosd, sind = cosine[count:], sine[count:]
    cosine, sine = cosine[:count], sine[:count]
    number = group * docs + jnp.arange(docs, dtype=jnp.int32)
    sel_in = (number[:, None] == request_docs[None, :]).astype(BF16)
    asked = lax.dynamic_slice_in_dim(request_docs, group * docs, docs, 0)
    sel_out = (asked[:, None] == jnp.arange(request_docs.shape[0], dtype=jnp.int32)[None, :]).astype(BF16)

    z, zd = down(
        x_pre.T, x_dec, wq_a, wkv_a, sel_in, q_gain.reshape(1, -1), kv_gain.reshape(1, -1),
        cosine.reshape(32, 16, 128), sine.reshape(32, 16, 128), cosd, sind,
    )
    o, od = attend(
        z.reshape(count, W), zd, wq_b, wkv_b, cosine, sine, cosd, sind,
        jnp.broadcast_to(seg[:, None], (count, 128)), jnp.broadcast_to(seg[None, :], (8, count)),
    )
    out_t, out_dec = up(o, od, wo, sel_out)
    return out_t.T, out_dec


def solution(mesh):
    placed = (
        P(("role", "grp"), "tp"),
        P(("role", "grp"), "tp"),
        P("tp", None),
        P("tp", None),
        P(),
        P(),
        P(None, "tp"),
        P(None, "tp"),
        P("tp", None),
        P(),
        P(),
    )
    return jax.shard_map(
        per_device,
        mesh=mesh,
        in_specs=placed,
        out_specs=(P(("role", "grp"), "tp"), P(("role", "grp"), "tp")),
        check_vma=False,
    )
```

time: 521 us -> 127 us (0.24)
  waiting for transfers between devices: 299 us -> 0 us
  blocking collectives: 123 us -> 0 us
  Pallas kernels: 0 us -> 112 us
  matrix products: 38.2 us -> 0 us
  local copies, waits for them, and re-layouts: 29 us -> 11.9 us
  between operations: 14.1 us -> 0.77 us
  other arithmetic: 15.3 us -> 2.31 us
    psum x1 -> x0, waiting for transfers between devices: 126 us -> none  [per_device(): lax.psum((part_q, part_kv, dpart_q, dpart_kv), 'tp')]
    psum x1 -> x0, blocking collectives: 123 us -> none  [per_device(): lax.psum((part_q, part_kv, dpart_q, dpart_kv), 'tp')]
    pallas_call x0 -> x3, Pallas kernels: none -> 112 us  [the longest x1 55.7 us: down(): pl.pallas_call(down_kernel, out_shape=(jax.ShapeDtypeStruct((NX, NY, 2, 1...]
    reduce_scatter x1 -> x0, waiting for transfers between devices: 98.4 us -> none  [per_device(): lax.psum_scatter(term_pre.astype(jnp.bfloat16), 'tp', scatter_dimension=1...]
    unnamed x5 -> x0, waiting for transfers between devices: 74.9 us -> none
    dot_general x19 -> x0, matrix products: 38.2 us -> none  [the longest x1 10.9 us: per_device(): term_pre = jnp.dot(o_pre, wo, preferred_element_type=jnp.float32)]
    gather x1 -> x0, local copies, waits for them, and re-layouts: 8.49 us -> none  [per_device(): cache = jnp.take(kv_all, index, axis=0)]
    all_gather x1 -> x0, local copies, waits for them, and re-layouts: 7.66 us -> none  [per_device(): kv_all = lax.all_gather(kv_row, ('role', 'grp'), axis=0, tiled=True)]
  transfers between devices with their start and end apart: 4 -> 0, of which waited for: 3 -> 0; matrix products, arithmetic and copies ran while one was open for 8% -> 0% of each run, Pallas kernels for 0% -> 0%
where the time goes in v1:
time: 127 us; the launch traced here: 126 us
  Pallas kernels  112 us (88%)
  local copies, waits for them, and re-layouts  11.9 us (9%)
  other arithmetic  2.31 us (2%)
    pallas_call x1, Pallas kernels, down(): pl.pallas_call(down_kernel, out_shape=(jax.ShapeDtypeStruct((NX, NY, 2, 1...  55.7 us
    pallas_call x1, Pallas kernels, up(): pl.pallas_call(up_kernel, out_shape=(jax.ShapeDtypeStruct((224, 512), BF1...  40.8 us
    pallas_call x1, Pallas kernels, attend(): pl.pallas_call(attend_kernel, out_shape=(jax.ShapeDtypeStruct((z.shape[0]...  15 us
    unnamed x8, local copies, waits for them, and re-layouts  3.19 us
    another operation x6, local copies, waits for them, and re-layouts, tables(): jnp.tile(cosine, (1, 4))  2.91 us
    another operation x6, local copies, waits for them, and re-layouts, tables(): jnp.tile(jnp.concatenate([-sine, sine], axis=1), (1, 2))  2.75 us

profile of v1, /device:TPU:1, one launch (start us, length us, event | category | flops | bytes accessed | tf_op | source)
XLA Modules:
  0.0 126.5 jit_solution(5787083939391741681)
XLA Ops:
  0.6 0.7 fusion.4
  1.3 0.1 copy.21
  1.5 0.1 reduce
  1.6 0.1 convert_reduce_fusion
  1.7 0.3 multiply_sine_fusion
  2.1 0.1 copy.29
  2.2 0.2 tile.32.clone
  2.4 0.0 copy-start.1
  2.4 0.0 copy-start
  2.4 1.0 tile.33.sin_ref
  3.4 0.1 copy.25
  3.5 0.7 tile.37.sind_ref
  4.2 0.3 multiply_cosine_fusion
  4.6 0.1 copy.28
  4.7 0.2 tile.30.clone
  4.9 1.2 tile.31.cos_ref
  6.1 0.1 copy.24
  6.1 0.7 tile.35.cosd_ref
  6.8 0.0 copy-done.1
  6.8 0.7 compare_convert_fusion.sel_ref
  7.5 0.0 copy-done
  7.5 0.6 reshape.134.qg_ref
  8.1 55.7 %down.1 = (bf16[4,4,2,16,2176]{4,3,2,1,0:T(8,128)(2,1)}, bf16[16,2176]{1,0:T(8,128)(2,1)}) custom-call(bf16[224,512]{1,0:T(8,128)(2,1)} %bitcast.17, bf16[16,224]{1,0:T(8,128)(2,1)} %xd_ref.1, bf16[224,1536]{1,0:T(8,128)(2,1)} %wqa_ref.1, bf16[224,576]{1,0:T(8,128)(2,1)} %wkva_ref.1, bf16[16,128]{1,0:T(8,128)(2,1)} %compare_convert_fusion.sel_ref, ...), custom_call_target="tpu_custom_call" | custom-call | tf_op jit(solution)/shard_map/down/pallas_call | solution.py:363
  63.8 0.8 copy.27.sin_ref
  64.7 0.8 copy.26.cos_ref
  65.5 0.8 broadcast_in_dim.21.segc_ref
  66.4 0.6 broadcast_in_dim.22.segr_ref
  67.0 15.0 %attend.1 = (bf16[512,512]{1,0:T(8,128)(2,1)}, bf16[16,512]{1,0:T(8,128)(2,1)}) custom-call(bf16[512,2176]{1,0:T(8,128)(2,1)} %bitcast.14, bf16[16,2176]{1,0:T(8,128)(2,1)} %get-tuple-element.9.zd_ref, bf16[1536,768]{1,0:T(8,128)(2,1)} %wqb_ref.1, bf16[512,1024]{1,0:T(8,128)(2,1)} %wkvb_ref.1, f32[512,128]{1,0:T(8,128)} %copy.26.cos_ref, ...), custom_call_target="tpu_custom_call" | custom-call | tf_op jit(solution)/shard_map/attend/pallas_call | solution.py:489
  82.0 0.1 dynamic_slice.7
  82.1 0.7 fusion.2.sel_ref
  82.7 40.8 %up.1 = (bf16[224,512]{1,0:T(8,128)(2,1)}, bf16[16,224]{1,0:T(8,128)(2,1)}) custom-call(bf16[512,512]{1,0:T(8,128)(2,1)} %get-tuple-element.10.o_ref, bf16[16,512]{1,0:T(8,128)(2,1)} %get-tuple-element.11.od_ref, bf16[512,7168]{1,0:T(8,128)(2,1)} %wo_ref.1, bf16[16,128]{1,0:T(8,128)(2,1)} %fusion.2.sel_ref), custom_call_target="tpu_custom_call" | custom-call | tf_op jit(solution)/shard_map/up/pallas_call | solution.py:632
  123.5 1.6 %copy.32 = bf16[512,224]{0,1:T(8,128)(2,1)} copy(bf16[512,224]{0,1:T(8,128)(2,1)} %bitcast.18) | data formatting | bytes 458752
  125.2 1.3 %copy.33 = bf16[16,224]{1,0:T(8,128)(2,1)} copy(bf16[16,224]{1,0:T(8,128)(2,1)} %get-tuple-element.23) | data formatting | bytes 14336
  (13 shorter events, 0.1 us)
Async XLA Ops:
  2.4 4.4 %copy-start.1 = (s32[128]{0:T(128)S(1)}, s32[128]{0:T(128)}, u32[]{:S(2)}) copy-start(s32[128]{0:T(128)} %param.21) | copy-start | bytes 1540
  2.4 5.1 %copy-start = (f32[1536]{0:T(1024)S(1)}, f32[1536]{0:T(1024)}, u32[]{:S(2)}) copy-start(f32[1536]{0:T(1024)} %param.15) | copy-start | bytes 18436

commit v2 on v1

v2 whole, which is shorter than its diff:
```python
import jax
import jax.numpy as jnp
import numpy as np
from jax import lax
from jax.experimental import pallas as pl
from jax.experimental.pallas import tpu as pltpu
from jax.sharding import PartitionSpec as P

QL = 1536
KL = 512
RD = 64
NOPE = 128
VD = 128
NX = 4
NY = 4
W = QL + KL + 128
SPLIT = 1152
EPS = 1e-06
F32 = jnp.float32
BF16 = jnp.bfloat16
MESH = pl.DeviceIdType.MESH
VMEM_LIMIT = 58 * 2**20


def place():
    tp = lax.axis_index("tp")
    return tp, tp // 8, lax.rem(tp // 2, NY), lax.rem(tp, 2)


def tp_of(x, y, c):
    return x * 8 + y * 2 + c


def next_of(p, step):
    return lax.rem(p + step + 4, 4)


def z_peer(step):
    z = lax.axis_index("role") * 2 + lax.axis_index("grp")
    other = lax.rem(z + step, 8)
    return z, other, {"role": other // 2, "grp": lax.rem(other, 2)}


def remote(src, dst, send, recv, device):
    return pltpu.make_async_remote_copy(
        src_ref=src, dst_ref=dst, send_sem=send, recv_sem=recv, device_id=device, device_id_type=MESH
    )


def chip_peer(x, y, c, step):
    other = lax.rem(x * 4 + y + step, 16)
    return other, {"tp": tp_of(other // 4, lax.rem(other, 4), c)}


def greet_start(x, y, c):
    barrier = pltpu.get_barrier_semaphore()
    pl.semaphore_signal(barrier, inc=1, device_id={"tp": tp_of(x, y, 1 - c)}, device_id_type=MESH)

    def chips(step, carry):
        _, device = chip_peer(x, y, c, step)
        pl.semaphore_signal(barrier, inc=1, device_id=device, device_id_type=MESH)
        return carry

    lax.fori_loop(1, 16, chips, 0)

    def planes(step, carry):
        _, _, device = z_peer(step)
        pl.semaphore_signal(barrier, inc=1, device_id=device, device_id_type=MESH)
        return carry

    lax.fori_loop(1, 8, planes, 0)


def greet_wait():
    pl.semaphore_wait(pltpu.get_barrier_semaphore(), 1 + 15 + 7)


class Ring:
    def __init__(self, data, near, far, part, pos, plus, minus, send, recv, base):
        self.data, self.near, self.far, self.part = data, near, far, part
        self.pos, self.plus, self.minus = pos, plus, minus
        self.send, self.recv, self.base = send, recv, base
        self.copies = {}

    def cut(self, ref, side):
        return ref.at[(Ellipsis, self.part[side])]

    def go(self, key, number, src, dst, device):
        copy = remote(src, dst, self.send.at[self.base + number], self.recv.at[self.base + number], device)
        copy.start()
        self.copies[key] = copy

    def start_far(self):
        chunk = self.data.at[next_of(self.pos, 2)]
        self.go("far0", 0, self.cut(chunk, 0), self.cut(self.far, 0), self.plus)
        self.go("far1", 1, self.cut(chunk, 1), self.cut(self.far, 1), self.minus)

    def start_near(self):
        up, down = self.data.at[next_of(self.pos, 1)], self.data.at[next_of(self.pos, -1)]
        self.go("up1", 2, self.cut(up, 1), self.cut(self.near.at[0], 1), self.plus)
        self.go("down0", 3, self.cut(down, 0), self.cut(self.near.at[1], 0), self.minus)

    def add(self, chunk, side):
        ref, extra = self.cut(chunk, side), self.cut(self.far, side)
        ref[...] = (ref[...].astype(F32) + extra[...].astype(F32)).astype(ref.dtype)

    def pass_on(self):
        up, down = self.data.at[next_of(self.pos, 1)], self.data.at[next_of(self.pos, -1)]
        self.copies["far0"].wait_recv()
        self.add(up, 0)
        self.go("up0", 4, self.cut(up, 0), self.cut(self.near.at[0], 0), self.plus)
        self.copies["far1"].wait_recv()
        self.add(down, 1)
        self.go("down1", 5, self.cut(down, 1), self.cut(self.near.at[1], 1), self.minus)

    def result(self, side):
        for key in ("up%d" % side, "down%d" % side):
            self.copies[key].wait_recv()
        own = self.cut(self.data.at[self.pos], side)[...].astype(F32)
        left = self.cut(self.near.at[0], side)[...].astype(F32)
        right = self.cut(self.near.at[1], side)[...].astype(F32)
        return own + (left + right)

    def close(self):
        for copy in self.copies.values():
            copy.wait_send()


def latent_rows(rows, q_gain, kv_gain, cosine, sine):
    q = rows[:, :QL]
    kv = rows[:, QL : QL + KL]
    turn = rows[:, QL + KL :]
    q = q * lax.rsqrt(jnp.mean(q * q, axis=-1, keepdims=True) + EPS) * q_gain
    kv = kv * lax.rsqrt(jnp.mean(kv * kv, axis=-1, keepdims=True) + EPS) * kv_gain
    turn = rope_tile(turn, cosine, sine)
    lane = lax.broadcasted_iota(jnp.int32, turn.shape, 1)
    turn = jnp.where(lane < RD, turn, 0.0)
    return q, kv, turn


def rope_tile(tile, cosine, sine):
    lane = lax.broadcasted_iota(jnp.int32, tile.shape, 1)
    swapped = jnp.where(lane % RD < RD // 2, pltpu.roll(tile, 96, 1), pltpu.roll(tile, 32, 1))
    return tile * cosine + swapped * sine


def turn_tables(pos, freq):
    turn = pos * freq
    lane = lax.broadcasted_iota(jnp.int32, turn.shape, 1)
    sine = jnp.sin(turn)
    return jnp.cos(turn), jnp.where(lane % RD < RD // 2, -sine, sine)


NT = (((1,), (1,)), ((), ()))
TN = (((0,), (0,)), ((), ()))


def split_query(query, cosine, sine):
    nope, rope = [], []
    lane = lax.broadcasted_iota(jnp.int32, (query.shape[0], 128), 1)
    for pair in range(query.shape[1] // 384):
        t0, t1, t2 = [query[:, 384 * pair + 128 * i : 384 * pair + 128 * i + 128] for i in range(3)]
        nope.append(t0.astype(BF16))
        nope.append(jnp.where(lane < 64, pltpu.roll(t1, 64, 1), pltpu.roll(t2, 64, 1)).astype(BF16))
        rope.append(rope_tile(jnp.where(lane < 64, t1, t2), cosine, sine).astype(BF16))
    return nope, rope


def whole_kernel(
    xt_ref, xd_ref, wqa_ref, wkva_ref, qg_ref, kvg_ref, freq_ref, len_ref, docs_ref, wqb_hbm, wkvb_hbm, wo_hbm,
    out_ref, outd_ref,
    wqb, wkvb, wo, wot, wkv_s, p0, p1, c0, c1, near0, near1, far0, far1, q0, q1, in0, in1,
    xd_all, dec, dec_in, tiles, tiles_in, sums_in, rows_in,
    zb, zd, pos_s, cos_s, sin_s, kv_s, o_s, od_s,
    t0, t1, tc0, tc1, tnear0, tnear1, tfar0, tfar1, tq0, tq1, tqnear0, tqnear1, tqfar0, tqfar1,
    dd, dt, dc, dn, dz,
    ws, zs, zr, cs, cr, rs, rr, ds, dr, es, er, gs, gr, ks, kr, ms, mr,
    us, ur, vs, vr, fs, fr, hs, hr, ys, yr,
):
    tp, x, y, c = place()
    chip = x * 4 + y
    z, _, _ = z_peer(0)
    peer = {"tp": tp_of(x, y, 1 - c)}
    xp, xm = {"tp": tp_of(next_of(x, 1), y, c)}, {"tp": tp_of(next_of(x, -1), y, c)}
    yp, ym = {"tp": tp_of(x, next_of(y, 1), c)}, {"tp": tp_of(x, next_of(y, -1), c)}
    greet_start(x, y, c)
    loads = [
        pltpu.make_async_copy(src, dst, ws.at[i])
        for i, (src, dst) in enumerate(((wo_hbm, wo), (wkvb_hbm, wkvb), (wqb_hbm, wqb)))
    ]
    for load in loads:
        load.start()

    wkv_s[...] = jnp.zeros_like(wkv_s)
    wkv_s[:, : KL + RD] = wkva_ref[...]
    order = (2, 1, 3, 0)
    core0, core1 = [], []
    for i, d in enumerate(order):
        xx = next_of(x, d)
        rows = xt_ref[:, pl.ds(pl.multiple_of(xx * 128, 128), 128)]
        for w_ref, lo, wide in ((wqa_ref, 0, QL), (wkv_s, QL, W - QL)):
            val = lax.dot_general(rows, w_ref[...], TN, preferred_element_type=F32)
            val = val.reshape(NY, 2, 2, 8, wide)
            for cc in range(2):
                p0[cc, xx, :, :, lo : lo + wide] = val[:, cc, 0]
                for yy in range(NY):
                    p1[cc, yy, xx, :, lo : lo + wide] = val[yy, cc, 1]
        if i == 0:
            greet_wait()
            xd_all[z] = xd_ref[...]

            def send_z(step, carry):
                zz, _, device = z_peer(step)
                remote(xd_ref, xd_all.at[zz], zs.at[step], zr.at[step], device).start()
                return carry

            lax.fori_loop(1, 8, send_z, 0)
        copy = remote(p0.at[1 - c, xx], c0.at[xx], cs.at[i], cr.at[i], peer)
        copy.start()
        core0.append(copy)
    for i, d in enumerate(order):
        yy = next_of(y, d)
        copy = remote(p1.at[1 - c, yy], c1.at[yy], cs.at[4 + i], cr.at[4 + i], peer)
        copy.start()
        core1.append(copy)

    own0, own1 = p0.at[c], p1.at[c]
    lanes = (slice(0, SPLIT), slice(SPLIT, W))
    ring0 = Ring(own0, near0, far0, lanes, x, xp, xm, rs, rr, 0)
    ring1 = Ring(own1, near1, far1, lanes, y, yp, ym, rs, rr, 6)
    both = ((ring0, own0, c0, core0, x), (ring1, own1, c1, core1, y))

    def take_core(i):
        for ring, own, came, copies, pos in both:
            copies[i].wait_recv()
            k = next_of(pos, order[i])
            own[k] = own[k] + came[k]

    take_core(0)
    ring0.start_far()
    ring1.start_far()
    take_core(1)
    take_core(2)
    ring0.start_near()
    ring1.start_near()
    take_core(3)

    def wait_z(step, carry):
        zz, other, device = z_peer(step)
        remote(xd_ref, xd_all.at[zz], zs.at[step], zr.at[step], device).wait()
        return carry

    lax.fori_loop(1, 8, wait_z, 0)
    ii = lax.broadcasted_iota(jnp.int32, (16, 128), 0)
    jj = lax.broadcasted_iota(jnp.int32, (16, 128), 1)
    docs = docs_ref[...].reshape(1, 128)
    sel_in = jnp.where(docs == z * 16 + ii, 1.0, 0.0).astype(BF16)
    asked = jnp.dot(sel_in, xd_all[...].reshape(128, -1), preferred_element_type=F32).astype(BF16)
    for w_ref, lo, wide in ((wqa_ref, 0, QL), (wkv_s, QL, W - QL)):
        val = jnp.dot(asked, w_ref[...], preferred_element_type=F32)
        dec[:, :, lo : lo + wide] = val.reshape(2, 8, wide)
    dec_core = remote(dec.at[1 - c], dec_in, ds.at[0], dr.at[0], peer)
    dec_core.start()

    lens = len_ref[pl.ds(z, 1), :].astype(F32)
    i16 = lax.broadcasted_iota(jnp.int32, (16, 16), 0)
    j16 = lax.broadcasted_iota(jnp.int32, (16, 16), 1)
    spread = jnp.broadcast_to(lens, (16, 16))
    len_col = jnp.sum(jnp.where(i16 == j16, spread, 0.0), axis=1, keepdims=True)
    end_col = jnp.sum(jnp.where(j16 <= i16, spread, 0.0), axis=1, keepdims=True)
    end_row = jnp.sum(jnp.where(i16 <= j16, jnp.broadcast_to(len_col, (16, 16)), 0.0), axis=0, keepdims=True)
    token = lax.broadcasted_iota(jnp.int32, (512, 16), 0).astype(F32)
    begun = jnp.sum(jnp.where(token >= end_row, jnp.broadcast_to(lens, (512, 16)), 0.0), axis=1, keepdims=True)
    pos = lax.broadcasted_iota(jnp.int32, (512, 128), 0).astype(F32) - begun
    pos_s[...] = pos
    freq = freq_ref[...]
    for i in range(4):
        part = pl.ds(128 * i, 128)
        cos_s[part, :], sin_s[part, :] = turn_tables(pos_s[part, :], freq)
    cosd, sind = turn_tables(jnp.broadcast_to(len_col, (16, 128)), freq)

    ring0.pass_on()
    ring1.pass_on()

    dec_core.wait()
    mine = dec[c] + dec_in[...]
    for j in range(16):
        tiles[j, :, 0:128] = mine[:, 128 * j : 128 * j + 128]
        tiles[j, :, 128:256] = mine[:, QL + KL :]

    def send_tile(step, carry):
        other, device = chip_peer(x, y, c, step)
        remote(tiles.at[other], tiles_in.at[chip], es.at[step], er.at[step], device).start()
        return carry

    lax.fori_loop(1, 16, send_tile, 0)
    tiles_in[chip] = tiles[chip]

    loads[0].wait()

    def turn_wo(k, carry):
        cut = pl.multiple_of(k * 896, 128)
        wot[pl.ds(cut, 896), :] = wo[:, pl.ds(cut, 896)].T
        return carry

    lax.fori_loop(0, 3, turn_wo, 0)

    for side in range(2):
        q0[:, :, lanes[side]] = ring0.result(side)
        q1[:, :, lanes[side]] = ring1.result(side)
    finals = []
    for h, (q, box, pos_h, dev) in enumerate(
        ((q0, in0, y, lambda d: tp_of(x, next_of(y, d), c)), (q1, in1, x, lambda d: tp_of(next_of(x, d), y, c)))
    ):
        for d in (2, 1, 3):
            n = 12 + 3 * h + d - 1
            copy = remote(q.at[next_of(pos_h, d)], box.at[d - 1], rs.at[n], rr.at[n], {"tp": dev(d)})
            copy.start()
            finals.append(copy)

    def wait_tile(step, carry):
        other, device = chip_peer(x, y, c, step)
        remote(tiles.at[other], tiles_in.at[chip], es.at[step], er.at[step], device).wait()
        return carry

    lax.fori_loop(1, 16, wait_tile, 0)
    total = jnp.sum(tiles_in[...], axis=0)
    sums_in[chip] = total[:, :128]

    def send_sum(step, carry):
        other, device = chip_peer(x, y, c, step)
        remote(sums_in.at[chip], sums_in.at[chip], gs.at[step], gr.at[step], device).start()
        return carry

    lax.fori_loop(1, 16, send_sum, 0)

    for copy in finals:
        copy.wait_recv()
    rows = jnp.concatenate(
        [q0[y] + (in0[0] + in0[1]) + in0[2], q1[x] + (in1[0] + in1[1]) + in1[2]], axis=0
    )
    own_rows = pl.ds(pl.multiple_of(tp * 16, 16), 16)
    q_gain, kv_gain = qg_ref[...].reshape(1, QL), kvg_ref[...].reshape(1, KL)
    q, kv, turn = latent_rows(rows, q_gain, kv_gain, cos_s[own_rows, :], sin_s[own_rows, :])
    zb[x, y, c, :, 0:QL] = q.astype(BF16)
    zb[x, y, c, :, QL : QL + KL] = kv.astype(BF16)
    zb[x, y, c, :, QL + KL : W] = turn.astype(BF16)

    copies = []
    ka, kb = slice(0, SPLIT), slice(SPLIT, W)
    every = slice(None)

    def push(block, device):
        n = len(copies)
        copy = remote(block, block, ks.at[n], kr.at[n], device)
        copy.start()
        copies.append(copy)
        return copy

    def along_x(d):
        return {"tp": tp_of(next_of(x, d), y, c)}

    def along_y(d):
        return {"tp": tp_of(x, next_of(y, d), c)}

    from_x, from_y = {}, {}
    for d in (1, 3, 2):
        from_x[d] = push(zb.at[x, y, c], along_x(d))
        from_y[d] = push(zb.at[x, y, c], along_y(d))
    diag_a, diag_b = [], []
    for d in (1, 3, 2):
        xn, yn = next_of(x, -d), next_of(y, -d)
        from_x[d].wait_recv()
        diag_a += [(e, push(zb.at[xn, y, c, :, ka], along_y(e))) for e in (1, 3, 2)]
        from_y[d].wait_recv()
        diag_b += [(e, push(zb.at[x, yn, c, :, kb], along_x(e))) for e in (1, 3, 2)]
    mates = [push(zb.at[:, y, c, :, ka], peer), push(zb.at[x, :, c, :, kb], peer)]

    def wait_sum(step, carry):
        other, device = chip_peer(x, y, c, step)
        remote(sums_in.at[chip], sums_in.at[chip], gs.at[step], gr.at[step], device).wait()
        return carry

    lax.fori_loop(1, 16, wait_sum, 0)
    for j in range(16):
        rows_in[c, :, 128 * j : 128 * j + 128] = sums_in[j]
    rows_in[c, :, QL + KL : W] = total[:, 128:]
    dec_mate = remote(rows_in.at[c], rows_in.at[c], ms.at[0], mr.at[0], peer)
    dec_mate.start()
    lax.fori_loop(3, 6, turn_wo, 0)
    dec_mate.wait()
    q, kv, turn = latent_rows(rows_in[...].reshape(16, W), q_gain, kv_gain, cosd, sind)
    zd[:, 0:QL] = q.astype(BF16)
    zd[:, QL : QL + KL] = kv.astype(BF16)
    zd[:, QL + KL : W] = turn.astype(BF16)
    lax.fori_loop(6, 8, turn_wo, 0)
    for e in (1, 3, 2):
        for number, copy in diag_a:
            if number == e:
                copy.wait_recv()
        mates.append(push(zb.at[:, next_of(y, -e), c, :, ka], peer))
        for number, copy in diag_b:
            if number == e:
                copy.wait_recv()
        mates.append(push(zb.at[next_of(x, -e), :, c, :, kb], peer))
    for load in loads[1:]:
        load.wait()
    for copy in mates:
        copy.wait_recv()

    heads = 4
    scale = 1.0 / float(NOPE + RD) ** 0.5
    wide = NOPE + VD

    def project(i, carry):
        kv = jnp.dot(zb[i, :, :, :, QL : QL + KL].reshape(128, KL), wkvb[...], preferred_element_type=F32)
        kv_s[pl.ds(pl.multiple_of(i * 128, 128), 128), :] = kv.astype(BF16)
        return carry

    def block(i, carry):
        first = pl.multiple_of(i * 128, 128)
        before = jnp.maximum(i - 1, 0)
        begin = pl.multiple_of(before * 128, 128)
        rows, keys = pl.ds(first, 128), pl.ds(begin, 256)
        query = jnp.dot(zb[i, :, :, :, :QL].reshape(128, QL), wqb[...], preferred_element_type=F32)
        nope, rope = split_query(query, cos_s[rows, :], sin_s[rows, :])
        turn = zb[pl.ds(before, 2), :, :, :, QL + KL : W].reshape(256, 128).astype(F32)
        turns = (turn.astype(BF16), pltpu.roll(turn, 64, 1).astype(BF16))
        own = first + lax.broadcasted_iota(jnp.int32, (128, 256), 0)
        other = begin + lax.broadcasted_iota(jnp.int32, (128, 256), 1)
        back = (own - other).astype(F32)
        keep = (back >= 0) & (back <= jnp.concatenate([pos_s[rows, :]] * 2, axis=1))
        for h in range(heads):
            q = jnp.concatenate([nope[h], rope[h // 2]], axis=1)
            k = jnp.concatenate([kv_s[keys, wide * h : wide * h + NOPE], turns[h % 2]], axis=1)
            s = lax.dot_general(q, k, NT, preferred_element_type=F32) * scale
            s = jnp.where(keep, s, -1e30)
            e = jnp.exp(s - jnp.max(s, axis=-1, keepdims=True))
            p = (e * (1.0 / jnp.sum(e, axis=-1, keepdims=True))).astype(BF16)
            v = kv_s[keys, wide * h + NOPE : wide * h + wide]
            o = jnp.dot(p, v, preferred_element_type=F32)
            o_s[rows, VD * h : VD * h + VD] = o.astype(BF16)
        return carry

    def decode():
        query = jnp.dot(zd[:, :QL], wqb[...], preferred_element_type=F32)
        nope, rope = split_query(query, cosd, sind)
        latent, own_lat = zb[..., QL : QL + KL].reshape(512, KL), zd[:, QL : QL + KL]
        turn, own_turn = zb[..., QL + KL : W].reshape(512, 128).astype(F32), zd[:, QL + KL : W].astype(F32)
        turns = (turn.astype(BF16), pltpu.roll(turn, 64, 1).astype(BF16))
        own_turns = (own_turn.astype(BF16), pltpu.roll(own_turn, 64, 1).astype(BF16))
        at = lax.broadcasted_iota(jnp.int32, (16, 512), 1).astype(F32)
        keep = (at < end_col) & (at >= end_col - len_col)
        diag = i16 == j16
        for h in range(heads):
            up_k = wkvb[:, wide * h : wide * h + NOPE]
            q_abs = lax.dot_general(nope[h], up_k, NT, preferred_element_type=F32).astype(BF16)
            s = lax.dot_general(q_abs, latent, NT, preferred_element_type=F32)
            s = (s + lax.dot_general(rope[h // 2], turns[h % 2], NT, preferred_element_type=F32)) * scale
            s = jnp.where(keep, s, -1e30)
            t = lax.dot_general(q_abs, own_lat, NT, preferred_element_type=F32)
            t = (t + lax.dot_general(rope[h // 2], own_turns[h % 2], NT, preferred_element_type=F32)) * scale
            t = jnp.where(diag, t, -1e30)
            top = jnp.maximum(jnp.max(s, axis=-1, keepdims=True), jnp.max(t, axis=-1, keepdims=True))
            e, f = jnp.exp(s - top), jnp.exp(t - top)
            part = 1.0 / (jnp.sum(e, axis=-1, keepdims=True) + jnp.sum(f, axis=-1, keepdims=True))
            lat = jnp.dot((e * part).astype(BF16), latent, preferred_element_type=F32)
            lat = lat + jnp.dot((f * part).astype(BF16), own_lat, preferred_element_type=F32)
            up_v = wkvb[:, wide * h + NOPE : wide * h + wide]
            o = jnp.dot(lat.astype(BF16), up_v, preferred_element_type=F32)
            od_s[:, VD * h : VD * h + VD] = o.astype(BF16)

    def output(s):
        def part(k, carry):
            xx, yy = k // 2, 2 * lax.rem(k, 2)
            w = wot[pl.ds(pl.multiple_of(k * 896, 128), 896), :]
            val = lax.dot_general(w, o_s[256 * s : 256 * s + 256, :], NT, preferred_element_type=F32).astype(BF16)
            for j in range(4):
                t0[s, j % 2, xx, yy + j // 2] = val[224 * j : 224 * j + 112]
                t1[s, j % 2, yy + j // 2, xx] = val[224 * j + 112 : 224 * j + 224]
            return carry

        lax.fori_loop(0, 8, part, 0)

    half = (slice(0, 128), slice(128, 256))

    class Stage:
        def __init__(self, s):
            self.s = s
            self.core = ([], [])
            self.rings = (
                Ring(t0.at[s, c], tnear0.at[s], tfar0.at[s], half, x, xp, xm, us, ur, 24 * s),
                Ring(t1.at[s, c], tnear1.at[s], tfar1.at[s], half, y, yp, ym, us, ur, 24 * s + 6),
            )
            self.lasts = (
                Ring(tq0.at[s], tqnear0.at[s], tqfar0.at[s], half, y, yp, ym, us, ur, 24 * s + 12),
                Ring(tq1.at[s], tqnear1.at[s], tqfar1.at[s], half, x, xp, xm, us, ur, 24 * s + 18),
            )
            self.parts = ((t0, tc0, x, self.core[0]), (t1, tc1, y, self.core[1]))

        def swap(self):
            for i, d in enumerate(order):
                for n, (t, came, pos_t, list_t) in enumerate(self.parts):
                    k, m = next_of(pos_t, d), 8 * self.s + 2 * i + n
                    copy = remote(t.at[self.s, 1 - c, k], came.at[self.s, k], vs.at[m], vr.at[m], peer)
                    copy.start()
                    list_t.append(copy)

        def take(self, i):
            for t, came, pos_t, list_t in self.parts:
                list_t[i].wait_recv()
                k = next_of(pos_t, order[i])
                t[self.s, c, k] = (t[self.s, c, k].astype(F32) + came[self.s, k].astype(F32)).astype(BF16)

        def first(self):
            self.take(0)
            for ring in self.rings:
                ring.start_far()
            self.take(1)
            self.take(2)
            for ring in self.rings:
                ring.start_near()
            self.take(3)

        def pass_on(self):
            for ring in self.rings:
                ring.pass_on()

        def second(self):
            for side in range(2):
                tq0[self.s, :, :, half[side]] = self.rings[0].result(side).astype(BF16)
                tq1[self.s, :, :, half[side]] = self.rings[1].result(side).astype(BF16)
            for ring in self.lasts:
                ring.start_far()
                ring.start_near()

        def pass_last(self):
            for ring in self.lasts:
                ring.pass_on()

        def finish(self):
            for h, ring in enumerate(self.lasts):
                for side in range(2):
                    at = 256 * self.s + 128 * side
                    out_ref[112 * h : 112 * h + 112, at : at + 128] = ring.result(side).astype(BF16)

        def close(self):
            for copy in self.core[0] + self.core[1]:
                copy.wait_send()
            for ring in self.rings + self.lasts:
                ring.close()

    s0, s1 = Stage(0), Stage(1)
    lax.fori_loop(0, 2, project, 0)
    lax.fori_loop(0, 2, block, 0)
    output(0)
    s0.swap()
    s0.first()
    decode()
    s0.pass_on()
    lax.fori_loop(2, 4, project, 0)
    lax.fori_loop(2, 4, block, 0)
    s0.second()
    output(1)
    s1.swap()

    dd[...] = jnp.zeros_like(dd)

    def dec_part(k, carry):
        w = wo[:, pl.ds(pl.multiple_of(k * 896, 128), 896)]
        dd[:, :896] = jnp.dot(od_s[...], w, preferred_element_type=F32)
        for j in range(4):
            at = 224 * j // 128 * 128
            v = dd[:, at : at + 384]
            if 224 * j - at:
                v = pltpu.roll(v, 384 - (224 * j - at), 1)
            dt[j % 2, 2 * k + j // 2] = v[:, :256].astype(BF16)
        return carry

    s0.pass_last()
    s1.first()
    lax.fori_loop(0, 8, dec_part, 0)
    dec_swap = remote(dt.at[1 - c], dc, fs.at[0], fr.at[0], peer)
    dec_swap.start()
    s0.finish()
    dec_swap.wait()
    dt[c] = (dt[c].astype(F32) + dc[...].astype(F32)).astype(BF16)

    def send_out(step, carry):
        other, device = chip_peer(x, y, c, step)
        remote(dt.at[c, other], dn.at[chip], hs.at[step], hr.at[step], device).start()
        return carry

    lax.fori_loop(1, 16, send_out, 0)
    dn[chip] = dt[c, chip]
    s1.pass_on()

    def wait_out(step, carry):
        other, device = chip_peer(x, y, c, step)
        remote(dt.at[c, other], dn.at[chip], hs.at[step], hr.at[step], device).wait()
        return carry

    lax.fori_loop(1, 16, wait_out, 0)
    dz[z] = jnp.sum(dn[...].astype(F32), axis=0).astype(BF16)

    def send_back(step, carry):
        zz, _, device = z_peer(step)
        remote(dz.at[zz], dz.at[zz], ys.at[step], yr.at[step], device).start()
        return carry

    lax.fori_loop(1, 8, send_back, 0)
    s1.second()

    def wait_back(step, carry):
        zz, _, device = z_peer(step)
        remote(dz.at[zz], dz.at[zz], ys.at[step], yr.at[step], device).wait()
        return carry

    lax.fori_loop(1, 8, wait_back, 0)
    wanted = jnp.sum(jnp.where(jj == z * 16 + ii, docs, 0).astype(F32), axis=1, keepdims=True)
    sel_out = jnp.where(jj.astype(F32) == wanted, 1.0, 0.0).astype(BF16)
    picked = jnp.dot(sel_out, dz[...].reshape(128, 256), preferred_element_type=F32)
    outd_ref[...] = picked[:, :224].astype(BF16)

    s1.pass_last()
    s1.finish()
    for copy in copies + core0 + core1 + finals:
        copy.wait_send()
    for ring in (ring0, ring1):
        ring.close()
    s0.close()
    s1.close()


def whole(xt, xd, wq_a, wkv_a, q_gain, kv_gain, freq, doc_len, docs, wq_b, wkv_b, wo):
    vm = pl.BlockSpec(memory_space=pltpu.VMEM)
    hbm = pl.BlockSpec(memory_space=pl.ANY)
    dma = pltpu.SemaphoreType.DMA
    shapes = [
        (wq_b.shape, BF16), (wkv_b.shape, BF16), (wo.shape, BF16), (wo.shape[::-1], BF16),
        ((wq_a.shape[0], W - QL), BF16),
        ((2, 4, 4, 8, W), F32), ((2, 4, 4, 8, W), F32), ((4, 4, 8, W), F32), ((4, 4, 8, W), F32),
        ((2, 4, 8, W), F32), ((2, 4, 8, W), F32), ((4, 8, W), F32), ((4, 8, W), F32),
        ((4, 8, W), F32), ((4, 8, W), F32), ((3, 8, W), F32), ((3, 8, W), F32),
        ((8,) + xd.shape, BF16), ((2, 8, W), F32), ((8, W), F32),
        ((16, 8, 256), F32), ((16, 8, 256), F32), ((16, 8, 128), F32), ((2, 8, W), F32),
        ((NX, NY, 2, 16, W), BF16), ((16, W), BF16), ((512, 128), F32), ((512, 128), F32), ((512, 128), F32),
        ((512, wkv_b.shape[1]), BF16), ((512, 512), BF16), ((16, 512), BF16),
        ((2, 2, 4, 4, 112, 256), BF16), ((2, 2, 4, 4, 112, 256), BF16),
        ((2, 4, 4, 112, 256), BF16), ((2, 4, 4, 112, 256), BF16),
        ((2, 2, 4, 112, 256), BF16), ((2, 2, 4, 112, 256), BF16),
        ((2, 4, 112, 256), BF16), ((2, 4, 112, 256), BF16),
        ((2, 4, 112, 256), BF16), ((2, 4, 112, 256), BF16),
        ((2, 2, 112, 256), BF16), ((2, 2, 112, 256), BF16),
        ((2, 112, 256), BF16), ((2, 112, 256), BF16),
        ((16, 1024), F32), ((2, 16, 16, 256), BF16), ((16, 16, 256), BF16), ((16, 16, 256), BF16),
        ((8, 16, 256), BF16),
    ]
    counts = (3, 8, 8, 8, 8, 18, 18, 1, 1, 16, 16, 16, 16, 32, 32, 1, 1, 48, 48, 16, 16, 1, 1, 16, 16, 8, 8)
    return pl.pallas_call(
        whole_kernel,
        out_shape=(jax.ShapeDtypeStruct((224, 512), BF16), jax.ShapeDtypeStruct((16, 224), BF16)),
        in_specs=[vm] * 9 + [hbm] * 3,
        out_specs=(vm, vm),
        scratch_shapes=[pltpu.VMEM(shape, kind) for shape, kind in shapes] + [dma((n,)) for n in counts],
        compiler_params=pltpu.CompilerParams(
            collective_id=0, has_side_effects=True, vmem_limit_bytes=VMEM_LIMIT
        ),
        name="whole",
    )(xt, xd, wq_a, wkv_a, q_gain, kv_gain, freq, doc_len, docs, wq_b, wkv_b, wo)


def per_device(x_pre, x_dec, wq_a, wkv_a, q_gain, kv_gain, wq_b, wkv_b, wo, doc_len, request_docs):
    half = RD // 2
    freq = np.tile(10000.0 ** (-np.arange(half) / half), 4).astype(np.float32)[None, :]
    out_t, out_dec = whole(
        x_pre.T, x_dec, wq_a, wkv_a, q_gain, kv_gain, jnp.asarray(freq), doc_len, request_docs, wq_b, wkv_b, wo
    )
    return out_t.T, out_dec


def solution(mesh):
    placed = (
        P(("role", "grp"), "tp"),
        P(("role", "grp"), "tp"),
        P("tp", None),
        P("tp", None),
        P(),
        P(),
        P(None, "tp"),
        P(None, "tp"),
        P("tp", None),
        P(),
        P(),
    )
    return jax.shard_map(
        per_device,
        mesh=mesh,
        in_specs=placed,
        out_specs=(P(("role", "grp"), "tp"), P(("role", "grp"), "tp")),
        check_vma=False,
    )
```

time: 127 us -> 97.8 us (0.77)
  Pallas kernels: 112 us -> 93.2 us
  local copies, waits for them, and re-layouts: 11.9 us -> 2.94 us
  other arithmetic: 2.31 us -> 0 us
    pallas_call x3 -> x1, Pallas kernels: 112 us -> 93.2 us  [whole(): pl.pallas_call(whole_kernel, out_shape=(jax.ShapeDtypeStruct((224, 512),...]
    another operation x14 -> x0, local copies, waits for them, and re-layouts: 6.44 us -> none  [the longest x6 2.91 us: tables(): jnp.tile(cosine, (1, 4))]
    broadcast_in_dim x2 -> x0, local copies, waits for them, and re-layouts: 1.44 us -> none  [the longest x1 0.83 us: per_device(): jnp.broadcast_to(seg[:, None], (count, 128))]
    convert_element_type x3 -> x0, other arithmetic: 1.34 us -> none  [the longest x1 0.67 us: per_device(): (asked[:, None] == jnp.arange(request_docs.shape[0], dtype=jnp.int32)[Non...]
    unnamed x8 -> x2, local copies, waits for them, and re-layouts: 3.19 us -> 2.94 us
where the time goes in v2:
time: 97.8 us; the launch traced here: 96.8 us
  Pallas kernels  93.2 us (95%)
  local copies, waits for them, and re-layouts  2.94 us (3%)
    pallas_call x1, Pallas kernels, whole(): pl.pallas_call(whole_kernel, out_shape=(jax.ShapeDtypeStruct((224, 512),...  93.2 us
    unnamed x2, local copies, waits for them, and re-layouts  2.94 us

profile of v2, /device:TPU:1, one launch (start us, length us, event | category | flops | bytes accessed | tf_op | source)
XLA Modules:
  0.0 96.8 jit_solution(11500938752484084405)
XLA Ops:
  0.6 93.2 %whole.1 = (bf16[224,512]{1,0:T(8,128)(2,1)}, bf16[16,224]{1,0:T(8,128)(2,1)}) custom-call(bf16[224,512]{1,0:T(8,128)(2,1)} %bitcast.3, bf16[16,224]{1,0:T(8,128)(2,1)} %xd_ref.1, bf16[224,1536]{1,0:T(8,128)(2,1)} %wqa_ref.1, bf16[224,576]{1,0:T(8,128)(2,1)} %wkva_ref.1, f32[1536]{0:T(1024)} %qg_ref.1, f32[512]{0:T(512)} %kvg_ref.1, ...), custom_call_target="tpu_custom_call" | custom-call | tf_op jit(solution)/shard_map/whole/pallas_call | solution.py:660
  93.8 1.6 %copy.16 = bf16[512,224]{0,1:T(8,128)(2,1)} copy(bf16[512,224]{0,1:T(8,128)(2,1)} %bitcast.2) | data formatting | bytes 458752
  95.5 1.3 %copy.17 = bf16[16,224]{1,0:T(8,128)(2,1)} copy(bf16[16,224]{1,0:T(8,128)(2,1)} %get-tuple-element.9) | data formatting | bytes 14336

commit v3 on v2

--- a/solution.py
+++ b/solution.py
@@ -171,8 +171,8 @@
     out_ref, outd_ref,
     wqb, wkvb, wo, wot, wkv_s, p0, p1, c0, c1, near0, near1, far0, far1, q0, q1, in0, in1,
     xd_all, dec, dec_in, tiles, tiles_in, sums_in, rows_in,
-    zb, zd, pos_s, cos_s, sin_s, kv_s, o_s, od_s,
-    t0, t1, tc0, tc1, tnear0, tnear1, tfar0, tfar1, tq0, tq1, tqnear0, tqnear1, tqfar0, tqfar1,
+    zb, zd, qabs_s, qrope_s, pos_s, cos_s, sin_s, kv_s, o_s, od_s,
+    t0, t1, tc0, tc1, tnear0, tnear1, tfar0, tfar1, tq0, tq1, tqin0, tqin1,
     dd, dt, dc, dn, dz,
     ws, zs, zr, cs, cr, rs, rr, ds, dr, es, er, gs, gr, ks, kr, ms, mr,
     us, ur, vs, vr, fs, fr, hs, hr, ys, yr,
@@ -195,6 +195,13 @@
     wkv_s[:, : KL + RD] = wkva_ref[...]
     order = (2, 1, 3, 0)
     core0, core1 = [], []
+
+    def swap_rows(i, p, came, pos_p, copies_p):
+        k, n = next_of(pos_p, order[i]), i if p is p0 else 4 + i
+        copy = remote(p.at[1 - c, k], came.at[k], cs.at[n], cr.at[n], peer)
+        copy.start()
+        copies_p.append(copy)
+
     for i, d in enumerate(order):
         xx = next_of(x, d)
         rows = xt_ref[:, pl.ds(pl.multiple_of(xx * 128, 128), 128)]
@@ -215,14 +222,11 @@
                 return carry
 
             lax.fori_loop(1, 8, send_z, 0)
-        copy = remote(p0.at[1 - c, xx], c0.at[xx], cs.at[i], cr.at[i], peer)
-        copy.start()
-        core0.append(copy)
-    for i, d in enumerate(order):
-        yy = next_of(y, d)
-        copy = remote(p1.at[1 - c, yy], c1.at[yy], cs.at[4 + i], cr.at[4 + i], peer)
-        copy.start()
-        core1.append(copy)
+            swap_rows(0, p0, c0, x, core0)
+    for i in range(4):
+        if i:
+            swap_rows(i, p0, c0, x, core0)
+        swap_rows(i, p1, c1, y, core1)
 
     own0, own1 = p0.at[c], p1.at[c]
     lanes = (slice(0, SPLIT), slice(SPLIT, W))
@@ -230,14 +234,16 @@
     ring1 = Ring(own1, near1, far1, lanes, y, yp, ym, rs, rr, 6)
     both = ((ring0, own0, c0, core0, x), (ring1, own1, c1, core1, y))
 
-    def take_core(i):
-        for ring, own, came, copies, pos in both:
-            copies[i].wait_recv()
-            k = next_of(pos, order[i])
-            own[k] = own[k] + came[k]
-
-    take_core(0)
+    def take_core(i, only=None):
+        for n, (ring, own, came, copies, pos) in enumerate(both):
+            if only in (None, n):
+                copies[i].wait_recv()
+                k = next_of(pos, order[i])
+                own[k] = own[k] + came[k]
+
+    take_core(0, 0)
     ring0.start_far()
+    take_core(0, 1)
     ring1.start_far()
     take_core(1)
     take_core(2)
@@ -363,10 +369,13 @@
     def along_y(d):
         return {"tp": tp_of(x, next_of(y, d), c)}
 
-    from_x, from_y = {}, {}
+    from_x, from_y, rest_x, rest_y = {}, {}, {}, {}
     for d in (1, 3, 2):
-        from_x[d] = push(zb.at[x, y, c], along_x(d))
-        from_y[d] = push(zb.at[x, y, c], along_y(d))
+        from_x[d] = push(zb.at[x, y, c, :, ka], along_x(d))
+        from_y[d] = push(zb.at[x, y, c, :, kb], along_y(d))
+    for d in (1, 3, 2):
+        rest_x[d] = push(zb.at[x, y, c, :, kb], along_x(d))
+        rest_y[d] = push(zb.at[x, y, c, :, ka], along_y(d))
     diag_a, diag_b = [], []
     for d in (1, 3, 2):
         xn, yn = next_of(x, -d), next_of(y, -d)
@@ -393,24 +402,31 @@
     zd[:, 0:QL] = q.astype(BF16)
     zd[:, QL : QL + KL] = kv.astype(BF16)
     zd[:, QL + KL : W] = turn.astype(BF16)
+    heads = 4
+    scale = 1.0 / float(NOPE + RD) ** 0.5
+    wide = NOPE + VD
+    for load in loads[1:]:
+        load.wait()
+    query = jnp.dot(zd[:, :QL], wqb[...], preferred_element_type=F32)
+    dec_nope, dec_rope = split_query(query, cosd, sind)
+    for h in range(heads):
+        up_k = wkvb[:, wide * h : wide * h + NOPE]
+        qabs_s[h] = lax.dot_general(dec_nope[h], up_k, NT, preferred_element_type=F32).astype(BF16)
+        qrope_s[h // 2] = dec_rope[h // 2]
     lax.fori_loop(6, 8, turn_wo, 0)
     for e in (1, 3, 2):
         for number, copy in diag_a:
             if number == e:
                 copy.wait_recv()
+        rest_y[e].wait_recv()
         mates.append(push(zb.at[:, next_of(y, -e), c, :, ka], peer))
         for number, copy in diag_b:
             if number == e:
                 copy.wait_recv()
+        rest_x[e].wait_recv()
         mates.append(push(zb.at[next_of(x, -e), :, c, :, kb], peer))
-    for load in loads[1:]:
-        load.wait()
     for copy in mates:
         copy.wait_recv()
-
-    heads = 4
-    scale = 1.0 / float(NOPE + RD) ** 0.5
-    wide = NOPE + VD
 
     def project(i, carry):
         kv = jnp.dot(zb[i, :, :, :, QL : QL + KL].reshape(128, KL), wkvb[...], preferred_element_type=F32)
@@ -443,8 +459,6 @@
         return carry
 
     def decode():
-        query = jnp.dot(zd[:, :QL], wqb[...], preferred_element_type=F32)
-        nope, rope = split_query(query, cosd, sind)
         latent, own_lat = zb[..., QL : QL + KL].reshape(512, KL), zd[:, QL : QL + KL]
         turn, own_turn = zb[..., QL + KL : W].reshape(512, 128).astype(F32), zd[:, QL + KL : W].astype(F32)
         turns = (turn.astype(BF16), pltpu.roll(turn, 64, 1).astype(BF16))
@@ -453,13 +467,12 @@
         keep = (at < end_col) & (at >= end_col - len_col)
         diag = i16 == j16
         for h in range(heads):
-            up_k = wkvb[:, wide * h : wide * h + NOPE]
-            q_abs = lax.dot_general(nope[h], up_k, NT, preferred_element_type=F32).astype(BF16)
+            q_abs, q_rope = qabs_s[h], qrope_s[h // 2]
             s = lax.dot_general(q_abs, latent, NT, preferred_element_type=F32)
-            s = (s + lax.dot_general(rope[h // 2], turns[h % 2], NT, preferred_element_type=F32)) * scale
+            s = (s + lax.dot_general(q_rope, turns[h % 2], NT, preferred_element_type=F32)) * scale
             s = jnp.where(keep, s, -1e30)
             t = lax.dot_general(q_abs, own_lat, NT, preferred_element_type=F32)
-            t = (t + lax.dot_general(rope[h // 2], own_turns[h % 2], NT, preferred_element_type=F32)) * scale
+            t = (t + lax.dot_general(q_rope, own_turns[h % 2], NT, preferred_element_type=F32)) * scale
             t = jnp.where(diag, t, -1e30)
             top = jnp.maximum(jnp.max(s, axis=-1, keepdims=True), jnp.max(t, axis=-1, keepdims=True))
             e, f = jnp.exp(s - top), jnp.exp(t - top)
@@ -471,7 +484,14 @@
             od_s[:, VD * h : VD * h + VD] = o.astype(BF16)
 
     def output(s):
-        def part(k, carry):
+        far_x, far_y = next_of(x, 2), next_of(y, 2) // 2
+
+        def part(n, carry):
+            k = jnp.where(
+                n < 2,
+                2 * far_x + n,
+                jnp.where(n < 5, 2 * next_of(far_x, n - 1) + far_y, 2 * next_of(far_x, n - 4) + 1 - far_y),
+            )
             xx, yy = k // 2, 2 * lax.rem(k, 2)
             w = wot[pl.ds(pl.multiple_of(k * 896, 128), 896), :]
             val = lax.dot_general(w, o_s[256 * s : 256 * s + 256, :], NT, preferred_element_type=F32).astype(BF16)
@@ -480,7 +500,7 @@
                 t1[s, j % 2, yy + j // 2, xx] = val[224 * j + 112 : 224 * j + 224]
             return carry
 
-        lax.fori_loop(0, 8, part, 0)
+        return part
 
     half = (slice(0, 128), slice(128, 256))
 
@@ -489,17 +509,19 @@
             self.s = s
             self.core = ([], [])
             self.rings = (
-                Ring(t0.at[s, c], tnear0.at[s], tfar0.at[s], half, x, xp, xm, us, ur, 24 * s),
-                Ring(t1.at[s, c], tnear1.at[s], tfar1.at[s], half, y, yp, ym, us, ur, 24 * s + 6),
+                Ring(t0.at[s, c], tnear0.at[s], tfar0.at[s], half, x, xp, xm, us, ur, 18 * s),
+                Ring(t1.at[s, c], tnear1.at[s], tfar1.at[s], half, y, yp, ym, us, ur, 18 * s + 6),
             )
-            self.lasts = (
-                Ring(tq0.at[s], tqnear0.at[s], tqfar0.at[s], half, y, yp, ym, us, ur, 24 * s + 12),
-                Ring(tq1.at[s], tqnear1.at[s], tqfar1.at[s], half, x, xp, xm, us, ur, 24 * s + 18),
-            )
+            self.lasts = [
+                (tq0, tqin0, y, lambda d: tp_of(x, next_of(y, d), c)),
+                (tq1, tqin1, x, lambda d: tp_of(next_of(x, d), y, c)),
+            ]
+            self.direct = ([], [])
             self.parts = ((t0, tc0, x, self.core[0]), (t1, tc1, y, self.core[1]))
 
-        def swap(self):
-            for i, d in enumerate(order):
+        def swap(self, which):
+            for i in which:
+                d = order[i]
                 for n, (t, came, pos_t, list_t) in enumerate(self.parts):
                     k, m = next_of(pos_t, d), 8 * self.s + 2 * i + n
                     copy = remote(t.at[self.s, 1 - c, k], came.at[self.s, k], vs.at[m], vr.at[m], peer)
@@ -530,39 +552,51 @@
             for side in range(2):
                 tq0[self.s, :, :, half[side]] = self.rings[0].result(side).astype(BF16)
                 tq1[self.s, :, :, half[side]] = self.rings[1].result(side).astype(BF16)
-            for ring in self.lasts:
-                ring.start_far()
-                ring.start_near()
-
-        def pass_last(self):
-            for ring in self.lasts:
-                ring.pass_on()
+            for d in (2, 1, 3):
+                for h, (data, box, pos_q, dev) in enumerate(self.lasts):
+                    n = 18 * self.s + 12 + 3 * h + d - 1
+                    copy = remote(
+                        data.at[self.s, next_of(pos_q, d)], box.at[self.s, d - 1], us.at[n], ur.at[n], {"tp": dev(d)}
+                    )
+                    copy.start()
+                    self.direct[h].append(copy)
 
         def finish(self):
-            for h, ring in enumerate(self.lasts):
-                for side in range(2):
-                    at = 256 * self.s + 128 * side
-                    out_ref[112 * h : 112 * h + 112, at : at + 128] = ring.result(side).astype(BF16)
+            for h, (data, box, pos_q, dev) in enumerate(self.lasts):
+                for copy in self.direct[h]:
+                    copy.wait_recv()
+                came = [box[self.s, i].astype(F32) for i in range(3)]
+                total = data[self.s, pos_q].astype(F32) + (came[0] + came[1]) + came[2]
+                out_ref[112 * h : 112 * h + 112, 256 * self.s : 256 * self.s + 256] = total.astype(BF16)
 
         def close(self):
             for copy in self.core[0] + self.core[1]:
                 copy.wait_send()
-            for ring in self.rings + self.lasts:
+            for ring in self.rings:
                 ring.close()
+            for copy in self.direct[0] + self.direct[1]:
+                copy.wait_send()
 
     s0, s1 = Stage(0), Stage(1)
+
+    def produce(stage):
+        part = output(stage.s)
+        lax.fori_loop(0, 5, part, 0)
+        stage.swap((0,))
+        lax.fori_loop(5, 8, part, 0)
+        stage.swap((1, 2, 3))
+
     lax.fori_loop(0, 2, project, 0)
     lax.fori_loop(0, 2, block, 0)
-    output(0)
-    s0.swap()
+    produce(s0)
     s0.first()
-    decode()
-    s0.pass_on()
     lax.fori_loop(2, 4, project, 0)
     lax.fori_loop(2, 4, block, 0)
+    s0.pass_on()
+    produce(s1)
+    s1.first()
     s0.second()
-    output(1)
-    s1.swap()
+    decode()
 
     dd[...] = jnp.zeros_like(dd)
 
@@ -577,11 +611,10 @@
             dt[j % 2, 2 * k + j // 2] = v[:, :256].astype(BF16)
         return carry
 
-    s0.pass_last()
-    s1.first()
     lax.fori_loop(0, 8, dec_part, 0)
     dec_swap = remote(dt.at[1 - c], dc, fs.at[0], fr.at[0], peer)
     dec_swap.start()
+    s1.pass_on()
     s0.finish()
     dec_swap.wait()
     dt[c] = (dt[c].astype(F32) + dc[...].astype(F32)).astype(BF16)
@@ -593,7 +626,6 @@
 
     lax.fori_loop(1, 16, send_out, 0)
     dn[chip] = dt[c, chip]
-    s1.pass_on()
 
     def wait_out(step, carry):
         other, device = chip_peer(x, y, c, step)
@@ -622,7 +654,6 @@
     picked = jnp.dot(sel_out, dz[...].reshape(128, 256), preferred_element_type=F32)
     outd_ref[...] = picked[:, :224].astype(BF16)
 
-    s1.pass_last()
     s1.finish()
     for copy in copies + core0 + core1 + finals:
         copy.wait_send()
@@ -644,19 +675,18 @@
         ((4, 8, W), F32), ((4, 8, W), F32), ((3, 8, W), F32), ((3, 8, W), F32),
         ((8,) + xd.shape, BF16), ((2, 8, W), F32), ((8, W), F32),
         ((16, 8, 256), F32), ((16, 8, 256), F32), ((16, 8, 128), F32), ((2, 8, W), F32),
-        ((NX, NY, 2, 16, W), BF16), ((16, W), BF16), ((512, 128), F32), ((512, 128), F32), ((512, 128), F32),
+        ((NX, NY, 2, 16, W), BF16), ((16, W), BF16), ((4, 16, KL), BF16), ((2, 16, 128), BF16), ((512, 128), F32), ((512, 128), F32), ((512, 128), F32),
         ((512, wkv_b.shape[1]), BF16), ((512, 512), BF16), ((16, 512), BF16),
         ((2, 2, 4, 4, 112, 256), BF16), ((2, 2, 4, 4, 112, 256), BF16),
         ((2, 4, 4, 112, 256), BF16), ((2, 4, 4, 112, 256), BF16),
         ((2, 2, 4, 112, 256), BF16), ((2, 2, 4, 112, 256), BF16),
         ((2, 4, 112, 256), BF16), ((2, 4, 112, 256), BF16),
         ((2, 4, 112, 256), BF16), ((2, 4, 112, 256), BF16),
-        ((2, 2, 112, 256), BF16), ((2, 2, 112, 256), BF16),
-        ((2, 112, 256), BF16), ((2, 112, 256), BF16),
+        ((2, 3, 112, 256), BF16), ((2, 3, 112, 256), BF16),
         ((16, 1024), F32), ((2, 16, 16, 256), BF16), ((16, 16, 256), BF16), ((16, 16, 256), BF16),
         ((8, 16, 256), BF16),
     ]
-    counts = (3, 8, 8, 8, 8, 18, 18, 1, 1, 16, 16, 16, 16, 32, 32, 1, 1, 48, 48, 16, 16, 1, 1, 16, 16, 8, 8)
+    counts = (3, 8, 8, 8, 8, 18, 18, 1, 1, 16, 16, 16, 16, 38, 38, 1, 1, 36, 36, 16, 16, 1, 1, 16, 16, 8, 8)
     return pl.pallas_call(
         whole_kernel,
         out_shape=(jax.ShapeDtypeStruct((224, 512), BF16), jax.ShapeDtypeStruct((16, 224), BF16)),
@@ -670,12 +700,29 @@
     )(xt, xd, wq_a, wkv_a, q_gain, kv_gain, freq, doc_len, docs, wq_b, wkv_b, wo)
 
 
+def hand_over_kernel(a_ref, b_ref, out_ref, outd_ref):
+    out_ref[...] = a_ref[...]
+    outd_ref[...] = b_ref[...]
+
+
+def hand_over(a, b):
+    vm = pl.BlockSpec(memory_space=pltpu.VMEM)
+    return pl.pallas_call(
+        hand_over_kernel,
+        out_shape=(jax.ShapeDtypeStruct(a.shape, a.dtype), jax.ShapeDtypeStruct(b.shape, b.dtype)),
+        in_specs=[vm, vm],
+        out_specs=(vm, vm),
+        name="hand_over",
+    )(a, b)
+
+
 def per_device(x_pre, x_dec, wq_a, wkv_a, q_gain, kv_gain, wq_b, wkv_b, wo, doc_len, request_docs):
     half = RD // 2
     freq = np.tile(10000.0 ** (-np.arange(half) / half), 4).astype(np.float32)[None, :]
     out_t, out_dec = whole(
         x_pre.T, x_dec, wq_a, wkv_a, q_gain, kv_gain, jnp.asarray(freq), doc_len, request_docs, wq_b, wkv_b, wo
     )
+    out_t, out_dec = hand_over(out_t, out_dec)
     return out_t.T, out_dec
 
 

time: 97.8 us -> 91.4 us (0.935)
  local copies, waits for them, and re-layouts: 2.94 us -> 0 us
  Pallas kernels: 93.2 us -> 90.7 us
    pallas_call x1, Pallas kernels: 93.2 us -> 89 us  [whole(): pl.pallas_call(whole_kernel, out_shape=(jax.ShapeDtypeStruct((224, 512),...]
    unnamed x2 -> x0, local copies, waits for them, and re-layouts: 2.94 us -> none
    pallas_call x0 -> x1, Pallas kernels: none -> 1.65 us  [hand_over(): pl.pallas_call(hand_over_kernel, out_shape=(jax.ShapeDtypeStruct(a.shape,...]
where the time goes in v3:
time: 91.4 us; the launch traced here: 91.3 us
  Pallas kernels  90.7 us (99%)
    pallas_call x1, Pallas kernels, whole(): pl.pallas_call(whole_kernel, out_shape=(jax.ShapeDtypeStruct((224, 512),...  89 us

profile of v3, /device:TPU:1, one launch (start us, length us, event | category | flops | bytes accessed | tf_op | source)
XLA Modules:
  0.0 91.3 jit_solution(10196734222397501702)
XLA Ops:
  0.6 89.0 %whole.1 = (bf16[224,512]{1,0:T(8,128)(2,1)}, bf16[16,224]{1,0:T(8,128)(2,1)}) custom-call(bf16[224,512]{1,0:T(8,128)(2,1)} %bitcast.2, bf16[16,224]{1,0:T(8,128)(2,1)} %xd_ref.1, bf16[224,1536]{1,0:T(8,128)(2,1)} %wqa_ref.1, bf16[224,576]{1,0:T(8,128)(2,1)} %wkva_ref.1, f32[1536]{0:T(1024)} %qg_ref.1, f32[512]{0:T(512)} %kvg_ref.1, ...), custom_call_target="tpu_custom_call" | custom-call | tf_op jit(solution)/shard_map/whole/pallas_call | solution.py:690
  89.7 1.6 %hand_over.1 = (bf16[224,512]{1,0:T(8,128)(2,1)}, bf16[16,224]{1,0:T(8,128)(2,1)}) custom-call(bf16[224,512]{1,0:T(8,128)(2,1)} %get-tuple-element.6.a_ref, bf16[16,224]{1,0:T(8,128)(2,1)} %get-tuple-element.7.b_ref), custom_call_target="tpu_custom_call" | custom-call | tf_op jit(solution)/shard_map/hand_over/pallas_call | solution.py:710

commit v4 on v3

--- a/solution.py
+++ b/solution.py
@@ -14,7 +14,8 @@
 NX = 4
 NY = 4
 W = QL + KL + 128
-SPLIT = 1152
+HALF = 1152
+SPLIT = 640
 EPS = 1e-06
 F32 = jnp.float32
 BF16 = jnp.bfloat16
@@ -76,10 +77,11 @@
 
 
 class Ring:
-    def __init__(self, data, near, far, part, pos, plus, minus, send, recv, base):
+    def __init__(self, data, near, far, part, pos, plus, minus, send, recv, base, sign=1):
         self.data, self.near, self.far, self.part = data, near, far, part
         self.pos, self.plus, self.minus = pos, plus, minus
         self.send, self.recv, self.base = send, recv, base
+        self.sign = sign
         self.copies = {}
 
     def cut(self, ref, side):
@@ -96,7 +98,7 @@
         self.go("far1", 1, self.cut(chunk, 1), self.cut(self.far, 1), self.minus)
 
     def start_near(self):
-        up, down = self.data.at[next_of(self.pos, 1)], self.data.at[next_of(self.pos, -1)]
+        up, down = self.data.at[next_of(self.pos, self.sign)], self.data.at[next_of(self.pos, -self.sign)]
         self.go("up1", 2, self.cut(up, 1), self.cut(self.near.at[0], 1), self.plus)
         self.go("down0", 3, self.cut(down, 0), self.cut(self.near.at[1], 0), self.minus)
 
@@ -105,7 +107,7 @@
         ref[...] = (ref[...].astype(F32) + extra[...].astype(F32)).astype(ref.dtype)
 
     def pass_on(self):
-        up, down = self.data.at[next_of(self.pos, 1)], self.data.at[next_of(self.pos, -1)]
+        up, down = self.data.at[next_of(self.pos, self.sign)], self.data.at[next_of(self.pos, -self.sign)]
         self.copies["far0"].wait_recv()
         self.add(up, 0)
         self.go("up0", 4, self.cut(up, 0), self.cut(self.near.at[0], 0), self.plus)
@@ -171,11 +173,12 @@
     out_ref, outd_ref,
     wqb, wkvb, wo, wot, wkv_s, p0, p1, c0, c1, near0, near1, far0, far1, q0, q1, in0, in1,
     xd_all, dec, dec_in, tiles, tiles_in, sums_in, rows_in,
-    zb, zd, qabs_s, qrope_s, pos_s, cos_s, sin_s, kv_s, o_s, od_s,
+    rows_s, square_s, square_in, gain_s,
+    zb, zd, qabs_s, qrope_s, pos_s, cos_s, sin_s, kv_s, turn_s, o_s, od_s,
     t0, t1, tc0, tc1, tnear0, tnear1, tfar0, tfar1, tq0, tq1, tqin0, tqin1,
     dd, dt, dc, dn, dz,
     ws, zs, zr, cs, cr, rs, rr, ds, dr, es, er, gs, gr, ks, kr, ms, mr,
-    us, ur, vs, vr, fs, fr, hs, hr, ys, yr,
+    us, ur, vs, vr, fs, fr, hs, hr, ys, yr, qs, qr,
 ):
     tp, x, y, c = place()
     chip = x * 4 + y
@@ -194,62 +197,179 @@
     wkv_s[...] = jnp.zeros_like(wkv_s)
     wkv_s[:, : KL + RD] = wkva_ref[...]
     order = (2, 1, 3, 0)
-    core0, core1 = [], []
-
-    def swap_rows(i, p, came, pos_p, copies_p):
-        k, n = next_of(pos_p, order[i]), i if p is p0 else 4 + i
-        copy = remote(p.at[1 - c, k], came.at[k], cs.at[n], cr.at[n], peer)
+    cut_q = 1024
+    sign = 1 - 2 * c
+
+    def product(s):
+        rows = xt_ref[:, 256 * s : 256 * s + 256]
+        for cc, w, lo in (
+            (0, wqa_ref[:, :cut_q], 0),
+            (1, wqa_ref[:, cut_q:], 0),
+            (1, wkv_s[...], QL - cut_q),
+        ):
+            wide = w.shape[1]
+            val = lax.dot_general(rows, w, TN, preferred_element_type=F32).reshape(NX, NY, 2, 8, wide)
+            p0[s, cc, :, :, :, lo : lo + wide] = val[:, :, 0]
+            for yy in range(NY):
+                p1[s, cc, yy, :, :, lo : lo + wide] = val[:, yy, 1]
+        p0[s, 0, :, :, :, cut_q:] = jnp.zeros((NX, NY, 8, HALF - cut_q), F32)
+        p1[s, 0, :, :, :, cut_q:] = jnp.zeros((NX, NY, 8, HALF - cut_q), F32)
+
+    lanes = (slice(0, SPLIT), slice(SPLIT, HALF))
+    ka, kb = lanes
+    copies = []
+
+    def push(block, device):
+        n = len(copies)
+        copy = remote(block, block, ks.at[n], kr.at[n], device)
         copy.start()
-        copies_p.append(copy)
-
-    for i, d in enumerate(order):
-        xx = next_of(x, d)
-        rows = xt_ref[:, pl.ds(pl.multiple_of(xx * 128, 128), 128)]
-        for w_ref, lo, wide in ((wqa_ref, 0, QL), (wkv_s, QL, W - QL)):
-            val = lax.dot_general(rows, w_ref[...], TN, preferred_element_type=F32)
-            val = val.reshape(NY, 2, 2, 8, wide)
-            for cc in range(2):
-                p0[cc, xx, :, :, lo : lo + wide] = val[:, cc, 0]
-                for yy in range(NY):
-                    p1[cc, yy, xx, :, lo : lo + wide] = val[yy, cc, 1]
-        if i == 0:
-            greet_wait()
-            xd_all[z] = xd_ref[...]
-
-            def send_z(step, carry):
-                zz, _, device = z_peer(step)
-                remote(xd_ref, xd_all.at[zz], zs.at[step], zr.at[step], device).start()
-                return carry
-
-            lax.fori_loop(1, 8, send_z, 0)
-            swap_rows(0, p0, c0, x, core0)
-    for i in range(4):
-        if i:
-            swap_rows(i, p0, c0, x, core0)
-        swap_rows(i, p1, c1, y, core1)
-
-    own0, own1 = p0.at[c], p1.at[c]
-    lanes = (slice(0, SPLIT), slice(SPLIT, W))
-    ring0 = Ring(own0, near0, far0, lanes, x, xp, xm, rs, rr, 0)
-    ring1 = Ring(own1, near1, far1, lanes, y, yp, ym, rs, rr, 6)
-    both = ((ring0, own0, c0, core0, x), (ring1, own1, c1, core1, y))
-
-    def take_core(i, only=None):
-        for n, (ring, own, came, copies, pos) in enumerate(both):
-            if only in (None, n):
-                copies[i].wait_recv()
-                k = next_of(pos, order[i])
-                own[k] = own[k] + came[k]
-
-    take_core(0, 0)
-    ring0.start_far()
-    take_core(0, 1)
-    ring1.start_far()
-    take_core(1)
-    take_core(2)
-    ring0.start_near()
-    ring1.start_near()
-    take_core(3)
+        copies.append(copy)
+        return copy
+
+    def along_x(d):
+        return {"tp": tp_of(next_of(x, d), y, c)}
+
+    def along_y(d):
+        return {"tp": tp_of(x, next_of(y, d), c)}
+
+    class Front:
+        def __init__(self, s):
+            self.s = s
+            self.core = ([], [])
+            self.parts = ((p0, c0, x, self.core[0]), (p1, c1, y, self.core[1]))
+            self.rings = (
+                Ring(
+                    p0.at[s, c], near0.at[s], far0.at[s], lanes, x, along_x(sign), along_x(-sign), rs, rr, 18 * s, sign
+                ),
+                Ring(
+                    p1.at[s, c], near1.at[s], far1.at[s], lanes, y, along_y(sign), along_y(-sign), rs, rr, 18 * s + 6,
+                    sign,
+                ),
+            )
+            self.direct = []
+
+        def swap(self):
+            for i, d in enumerate(order):
+                for h, (p, came, pos_p, list_p) in enumerate(self.parts):
+                    k, n = next_of(pos_p, d), 8 * self.s + 2 * i + h
+                    copy = remote(p.at[self.s, 1 - c, k], came.at[self.s, k], cs.at[n], cr.at[n], peer)
+                    copy.start()
+                    list_p.append(copy)
+
+        def take(self, i, h):
+            p, came, pos_p, list_p = self.parts[h]
+            list_p[i].wait_recv()
+            k = next_of(pos_p, order[i])
+            p[self.s, c, k] = p[self.s, c, k] + came[self.s, k]
+
+        def first(self):
+            for h in range(2):
+                self.take(0, h)
+                self.rings[h].start_far()
+            for h in range(2):
+                self.take(1, h)
+                self.take(2, h)
+                self.rings[h].start_near()
+            for h in range(2):
+                self.take(3, h)
+
+        def pass_on(self):
+            for ring in self.rings:
+                ring.pass_on()
+
+        def second(self):
+            for h, (q, box, pos_h, dev) in enumerate(((q0, in0, y, along_y), (q1, in1, x, along_x))):
+                for side in range(2):
+                    q[self.s, :, :, lanes[side]] = self.rings[h].result(side)
+                for d in (2, 1, 3):
+                    n = 18 * self.s + 12 + 3 * h + d - 1
+                    copy = remote(
+                        q.at[self.s, next_of(pos_h, d)], box.at[self.s, d - 1], rs.at[n], rr.at[n], dev(d)
+                    )
+                    copy.start()
+                    self.direct.append(copy)
+
+        def rows(self):
+            for copy in self.direct:
+                copy.wait_recv()
+            s = self.s
+            top = q0[s, y] + (in0[s, 0] + in0[s, 1]) + in0[s, 2]
+            low = q1[s, x] + (in1[s, 0] + in1[s, 1]) + in1[s, 2]
+            rows = jnp.concatenate([top, low], axis=0)
+            rows_s[s] = rows
+            left = jnp.sum(rows[:, :512] * rows[:, :512], axis=-1, keepdims=True)
+            right = jnp.sum(rows[:, 512:cut_q] * rows[:, 512:cut_q], axis=-1, keepdims=True)
+            square_s[s, 0] = jnp.broadcast_to(left + jnp.where(c == 0, right, 0.0), (16, 128))
+            square_s[s, 1] = jnp.broadcast_to(right, (16, 128))
+            self.square = remote(square_s.at[s, 0], square_in.at[s], qs.at[s], qr.at[s], peer)
+            self.square.start()
+
+        def norm(self):
+            s = self.s
+            self.square.wait_recv()
+            rows = rows_s[s]
+            mean_q = (square_s[s, 0] + square_in[s])[:, 0:1] * (1.0 / QL)
+            mean_kv = square_s[s, 1][:, 0:1] * (1.0 / KL)
+            scale_q, scale_kv = lax.rsqrt(mean_q + EPS), lax.rsqrt(mean_kv + EPS)
+            gain = gain_s[pl.ds(c, 1), :]
+            at = pl.ds(pl.multiple_of(256 * s + 16 * chip, 16), 16)
+            turn = rope_tile(rows[:, cut_q:], cos_s[at, :], sin_s[at, :])
+            lane = lax.broadcasted_iota(jnp.int32, turn.shape, 1)
+            zb[s, c, x, y, :, 0:512] = (rows[:, :512] * scale_q * gain[:, :512]).astype(BF16)
+            both = jnp.where(c == 0, scale_q, scale_kv)
+            zb[s, c, x, y, :, 512:cut_q] = (rows[:, 512:cut_q] * both * gain[:, 512:cut_q]).astype(BF16)
+            zb[s, c, x, y, :, cut_q:] = jnp.where(lane < RD, turn, 0.0).astype(BF16)
+
+        def gather_one(self):
+            s = self.s
+            self.one = []
+            for d in (1, 3, 2):
+                self.one.append(push(zb.at[s, c, x, y, :, ka], along_x(d)))
+                self.one.append(push(zb.at[s, c, x, y, :, kb], along_y(d)))
+
+        def gather_two(self):
+            s = self.s
+            self.two_a, self.two_b = [], []
+            for copy in self.one:
+                copy.wait_recv()
+            for d in (1, 3, 2):
+                self.two_a.append(push(zb.at[s, c, :, y, :, ka], along_y(d)))
+                self.two_b.append(push(zb.at[s, c, x, :, :, kb], along_x(d)))
+
+        def gather_mate(self):
+            for copy in self.two_a:
+                copy.wait_recv()
+            self.mates = [push(zb.at[self.s, c, :, :, :, ka], peer)]
+            for copy in self.two_b:
+                copy.wait_recv()
+            self.mates.append(push(zb.at[self.s, c, :, :, :, kb], peer))
+
+        def gather_end(self):
+            for copy in self.mates:
+                copy.wait_recv()
+
+        def close(self):
+            for copy in self.core[0] + self.core[1] + self.direct + [self.square]:
+                copy.wait_send()
+            for ring in self.rings:
+                ring.close()
+
+    f0, f1 = Front(0), Front(1)
+    product(0)
+    greet_wait()
+    f0.swap()
+    xd_all[z] = xd_ref[...]
+
+    def send_z(step, carry):
+        zz, _, device = z_peer(step)
+        remote(xd_ref, xd_all.at[zz], zs.at[step], zr.at[step], device).start()
+        return carry
+
+    lax.fori_loop(1, 8, send_z, 0)
+    product(1)
+    f1.swap()
+    f0.first()
+    f1.first()
 
     def wait_z(step, carry):
         zz, other, device = z_peer(step)
@@ -267,7 +387,13 @@
         dec[:, :, lo : lo + wide] = val.reshape(2, 8, wide)
     dec_core = remote(dec.at[1 - c], dec_in, ds.at[0], dr.at[0], peer)
     dec_core.start()
-
+    f0.pass_on()
+
+    q_gain, kv_gain = qg_ref[...].reshape(1, QL), kvg_ref[...].reshape(1, KL)
+    gain_s[...] = jnp.zeros_like(gain_s)
+    gain_s[0:1, :cut_q] = q_gain[:, :cut_q]
+    gain_s[1:2, : QL - cut_q] = q_gain[:, cut_q:]
+    gain_s[1:2, QL - cut_q : cut_q] = kv_gain
     lens = len_ref[pl.ds(z, 1), :].astype(F32)
     i16 = lax.broadcasted_iota(jnp.int32, (16, 16), 0)
     j16 = lax.broadcasted_iota(jnp.int32, (16, 16), 1)
@@ -285,9 +411,6 @@
         cos_s[part, :], sin_s[part, :] = turn_tables(pos_s[part, :], freq)
     cosd, sind = turn_tables(jnp.broadcast_to(len_col, (16, 128)), freq)
 
-    ring0.pass_on()
-    ring1.pass_on()
-
     dec_core.wait()
     mine = dec[c] + dec_in[...]
     for j in range(16):
@@ -302,6 +425,8 @@
     lax.fori_loop(1, 16, send_tile, 0)
     tiles_in[chip] = tiles[chip]
 
+    f0.second()
+    f1.pass_on()
     loads[0].wait()
 
     def turn_wo(k, carry):
@@ -309,21 +434,6 @@
         wot[pl.ds(cut, 896), :] = wo[:, pl.ds(cut, 896)].T
         return carry
 
-    lax.fori_loop(0, 3, turn_wo, 0)
-
-    for side in range(2):
-        q0[:, :, lanes[side]] = ring0.result(side)
-        q1[:, :, lanes[side]] = ring1.result(side)
-    finals = []
-    for h, (q, box, pos_h, dev) in enumerate(
-        ((q0, in0, y, lambda d: tp_of(x, next_of(y, d), c)), (q1, in1, x, lambda d: tp_of(next_of(x, d), y, c)))
-    ):
-        for d in (2, 1, 3):
-            n = 12 + 3 * h + d - 1
-            copy = remote(q.at[next_of(pos_h, d)], box.at[d - 1], rs.at[n], rr.at[n], {"tp": dev(d)})
-            copy.start()
-            finals.append(copy)
-
     def wait_tile(step, carry):
         other, device = chip_peer(x, y, c, step)
         remote(tiles.at[other], tiles_in.at[chip], es.at[step], er.at[step], device).wait()
@@ -339,51 +449,10 @@
         return carry
 
     lax.fori_loop(1, 16, send_sum, 0)
-
-    for copy in finals:
-        copy.wait_recv()
-    rows = jnp.concatenate(
-        [q0[y] + (in0[0] + in0[1]) + in0[2], q1[x] + (in1[0] + in1[1]) + in1[2]], axis=0
-    )
-    own_rows = pl.ds(pl.multiple_of(tp * 16, 16), 16)
-    q_gain, kv_gain = qg_ref[...].reshape(1, QL), kvg_ref[...].reshape(1, KL)
-    q, kv, turn = latent_rows(rows, q_gain, kv_gain, cos_s[own_rows, :], sin_s[own_rows, :])
-    zb[x, y, c, :, 0:QL] = q.astype(BF16)
-    zb[x, y, c, :, QL : QL + KL] = kv.astype(BF16)
-    zb[x, y, c, :, QL + KL : W] = turn.astype(BF16)
-
-    copies = []
-    ka, kb = slice(0, SPLIT), slice(SPLIT, W)
-    every = slice(None)
-
-    def push(block, device):
-        n = len(copies)
-        copy = remote(block, block, ks.at[n], kr.at[n], device)
-        copy.start()
-        copies.append(copy)
-        return copy
-
-    def along_x(d):
-        return {"tp": tp_of(next_of(x, d), y, c)}
-
-    def along_y(d):
-        return {"tp": tp_of(x, next_of(y, d), c)}
-
-    from_x, from_y, rest_x, rest_y = {}, {}, {}, {}
-    for d in (1, 3, 2):
-        from_x[d] = push(zb.at[x, y, c, :, ka], along_x(d))
-        from_y[d] = push(zb.at[x, y, c, :, kb], along_y(d))
-    for d in (1, 3, 2):
-        rest_x[d] = push(zb.at[x, y, c, :, kb], along_x(d))
-        rest_y[d] = push(zb.at[x, y, c, :, ka], along_y(d))
-    diag_a, diag_b = [], []
-    for d in (1, 3, 2):
-        xn, yn = next_of(x, -d), next_of(y, -d)
-        from_x[d].wait_recv()
-        diag_a += [(e, push(zb.at[xn, y, c, :, ka], along_y(e))) for e in (1, 3, 2)]
-        from_y[d].wait_recv()
-        diag_b += [(e, push(zb.at[x, yn, c, :, kb], along_x(e))) for e in (1, 3, 2)]
-    mates = [push(zb.at[:, y, c, :, ka], peer), push(zb.at[x, :, c, :, kb], peer)]
+    f0.rows()
+    f1.second()
+    f0.norm()
+    f0.gather_one()
 
     def wait_sum(step, carry):
         other, device = chip_peer(x, y, c, step)
@@ -396,7 +465,10 @@
     rows_in[c, :, QL + KL : W] = total[:, 128:]
     dec_mate = remote(rows_in.at[c], rows_in.at[c], ms.at[0], mr.at[0], peer)
     dec_mate.start()
-    lax.fori_loop(3, 6, turn_wo, 0)
+    f1.rows()
+    f0.gather_two()
+    f1.norm()
+    f1.gather_one()
     dec_mate.wait()
     q, kv, turn = latent_rows(rows_in[...].reshape(16, W), q_gain, kv_gain, cosd, sind)
     zd[:, 0:QL] = q.astype(BF16)
@@ -413,55 +485,55 @@
         up_k = wkvb[:, wide * h : wide * h + NOPE]
         qabs_s[h] = lax.dot_general(dec_nope[h], up_k, NT, preferred_element_type=F32).astype(BF16)
         qrope_s[h // 2] = dec_rope[h // 2]
-    lax.fori_loop(6, 8, turn_wo, 0)
-    for e in (1, 3, 2):
-        for number, copy in diag_a:
-            if number == e:
-                copy.wait_recv()
-        rest_y[e].wait_recv()
-        mates.append(push(zb.at[:, next_of(y, -e), c, :, ka], peer))
-        for number, copy in diag_b:
-            if number == e:
-                copy.wait_recv()
-        rest_x[e].wait_recv()
-        mates.append(push(zb.at[next_of(x, -e), :, c, :, kb], peer))
-    for copy in mates:
-        copy.wait_recv()
-
-    def project(i, carry):
-        kv = jnp.dot(zb[i, :, :, :, QL : QL + KL].reshape(128, KL), wkvb[...], preferred_element_type=F32)
-        kv_s[pl.ds(pl.multiple_of(i * 128, 128), 128), :] = kv.astype(BF16)
-        return carry
-
-    def block(i, carry):
-        first = pl.multiple_of(i * 128, 128)
-        before = jnp.maximum(i - 1, 0)
-        begin = pl.multiple_of(before * 128, 128)
-        rows, keys = pl.ds(first, 128), pl.ds(begin, 256)
-        query = jnp.dot(zb[i, :, :, :, :QL].reshape(128, QL), wqb[...], preferred_element_type=F32)
-        nope, rope = split_query(query, cos_s[rows, :], sin_s[rows, :])
-        turn = zb[pl.ds(before, 2), :, :, :, QL + KL : W].reshape(256, 128).astype(F32)
-        turns = (turn.astype(BF16), pltpu.roll(turn, 64, 1).astype(BF16))
-        own = first + lax.broadcasted_iota(jnp.int32, (128, 256), 0)
-        other = begin + lax.broadcasted_iota(jnp.int32, (128, 256), 1)
-        back = (own - other).astype(F32)
-        keep = (back >= 0) & (back <= jnp.concatenate([pos_s[rows, :]] * 2, axis=1))
-        for h in range(heads):
-            q = jnp.concatenate([nope[h], rope[h // 2]], axis=1)
-            k = jnp.concatenate([kv_s[keys, wide * h : wide * h + NOPE], turns[h % 2]], axis=1)
-            s = lax.dot_general(q, k, NT, preferred_element_type=F32) * scale
-            s = jnp.where(keep, s, -1e30)
-            e = jnp.exp(s - jnp.max(s, axis=-1, keepdims=True))
-            p = (e * (1.0 / jnp.sum(e, axis=-1, keepdims=True))).astype(BF16)
-            v = kv_s[keys, wide * h + NOPE : wide * h + wide]
-            o = jnp.dot(p, v, preferred_element_type=F32)
-            o_s[rows, VD * h : VD * h + VD] = o.astype(BF16)
-        return carry
+    f1.gather_two()
+    lax.fori_loop(0, 4, turn_wo, 0)
+    f0.gather_mate()
+    lax.fori_loop(4, 8, turn_wo, 0)
+    f0.gather_end()
+
+    def project(s):
+        rows = slice(256 * s, 256 * s + 256)
+        latent = zb[s, 1, :, :, :, QL - cut_q : cut_q].reshape(256, KL)
+        kv_s[rows, :] = jnp.dot(latent, wkvb[...], preferred_element_type=F32).astype(BF16)
+        turn = zb[s, 1, :, :, :, cut_q:].reshape(256, 128)
+        turn_s[0, rows, :] = turn
+        turn_s[1, rows, :] = pltpu.roll(turn.astype(F32), 64, 1).astype(BF16)
+
+    def block(s):
+        def attend(j, carry):
+            i = 2 * s + j
+            first = pl.multiple_of(i * 128, 128)
+            begin = pl.multiple_of(jnp.maximum(i - 1, 0) * 128, 128)
+            rows, keys = pl.ds(first, 128), pl.ds(begin, 256)
+            chips = pl.ds(2 * j, 2)
+            query = jnp.dot(
+                zb[s, 0, chips, :, :, :cut_q].reshape(128, cut_q), wqb[:cut_q, :], preferred_element_type=F32
+            )
+            query = query + jnp.dot(
+                zb[s, 1, chips, :, :, : QL - cut_q].reshape(128, QL - cut_q), wqb[cut_q:, :], preferred_element_type=F32
+            )
+            nope, rope = split_query(query, cos_s[rows, :], sin_s[rows, :])
+            own = first + lax.broadcasted_iota(jnp.int32, (128, 256), 0)
+            other = begin + lax.broadcasted_iota(jnp.int32, (128, 256), 1)
+            back = (own - other).astype(F32)
+            keep = (back >= 0) & (back <= jnp.concatenate([pos_s[rows, :]] * 2, axis=1))
+            for h in range(heads):
+                q = jnp.concatenate([nope[h], rope[h // 2]], axis=1)
+                k = jnp.concatenate([kv_s[keys, wide * h : wide * h + NOPE], turn_s[h % 2, keys, :]], axis=1)
+                s_h = lax.dot_general(q, k, NT, preferred_element_type=F32) * scale
+                s_h = jnp.where(keep, s_h, -1e30)
+                e = jnp.exp(s_h - jnp.max(s_h, axis=-1, keepdims=True))
+                p = (e * (1.0 / jnp.sum(e, axis=-1, keepdims=True))).astype(BF16)
+                v = kv_s[keys, wide * h + NOPE : wide * h + wide]
+                o = jnp.dot(p, v, preferred_element_type=F32)
+                o_s[rows, VD * h : VD * h + VD] = o.astype(BF16)
+            return carry
+
+        lax.fori_loop(0, 2, attend, 0)
 
     def decode():
-        latent, own_lat = zb[..., QL : QL + KL].reshape(512, KL), zd[:, QL : QL + KL]
-        turn, own_turn = zb[..., QL + KL : W].reshape(512, 128).astype(F32), zd[:, QL + KL : W].astype(F32)
-        turns = (turn.astype(BF16), pltpu.roll(turn, 64, 1).astype(BF16))
+        latent, own_lat = zb[:, 1, :, :, :, QL - cut_q : cut_q].reshape(512, KL), zd[:, QL : QL + KL]
+        turns, own_turn = (turn_s[0], turn_s[1]), zd[:, QL + KL : W].astype(F32)
         own_turns = (own_turn.astype(BF16), pltpu.roll(own_turn, 64, 1).astype(BF16))
         at = lax.broadcasted_iota(jnp.int32, (16, 512), 1).astype(F32)
         keep = (at < end_col) & (at >= end_col - len_col)
@@ -586,12 +658,14 @@
         lax.fori_loop(5, 8, part, 0)
         stage.swap((1, 2, 3))
 
-    lax.fori_loop(0, 2, project, 0)
-    lax.fori_loop(0, 2, block, 0)
+    project(0)
+    block(0)
+    f1.gather_mate()
     produce(s0)
     s0.first()
-    lax.fori_loop(2, 4, project, 0)
-    lax.fori_loop(2, 4, block, 0)
+    f1.gather_end()
+    project(1)
+    block(1)
     s0.pass_on()
     produce(s1)
     s1.first()
@@ -655,10 +729,10 @@
     outd_ref[...] = picked[:, :224].astype(BF16)
 
     s1.finish()
-    for copy in copies + core0 + core1 + finals:
+    for copy in copies:
         copy.wait_send()
-    for ring in (ring0, ring1):
-        ring.close()
+    f0.close()
+    f1.close()
     s0.close()
     s1.close()
 
@@ -670,13 +744,17 @@
     shapes = [
         (wq_b.shape, BF16), (wkv_b.shape, BF16), (wo.shape, BF16), (wo.shape[::-1], BF16),
         ((wq_a.shape[0], W - QL), BF16),
-        ((2, 4, 4, 8, W), F32), ((2, 4, 4, 8, W), F32), ((4, 4, 8, W), F32), ((4, 4, 8, W), F32),
-        ((2, 4, 8, W), F32), ((2, 4, 8, W), F32), ((4, 8, W), F32), ((4, 8, W), F32),
-        ((4, 8, W), F32), ((4, 8, W), F32), ((3, 8, W), F32), ((3, 8, W), F32),
+        ((2, 2, 4, 4, 8, HALF), F32), ((2, 2, 4, 4, 8, HALF), F32),
+        ((2, 4, 4, 8, HALF), F32), ((2, 4, 4, 8, HALF), F32),
+        ((2, 2, 4, 8, HALF), F32), ((2, 2, 4, 8, HALF), F32),
+        ((2, 4, 8, HALF), F32), ((2, 4, 8, HALF), F32),
+        ((2, 4, 8, HALF), F32), ((2, 4, 8, HALF), F32),
+        ((2, 3, 8, HALF), F32), ((2, 3, 8, HALF), F32),
         ((8,) + xd.shape, BF16), ((2, 8, W), F32), ((8, W), F32),
         ((16, 8, 256), F32), ((16, 8, 256), F32), ((16, 8, 128), F32), ((2, 8, W), F32),
-        ((NX, NY, 2, 16, W), BF16), ((16, W), BF16), ((4, 16, KL), BF16), ((2, 16, 128), BF16), ((512, 128), F32), ((512, 128), F32), ((512, 128), F32),
-        ((512, wkv_b.shape[1]), BF16), ((512, 512), BF16), ((16, 512), BF16),
+        ((2, 16, HALF), F32), ((2, 2, 16, 128), F32), ((2, 16, 128), F32), ((8, HALF), F32),
+        ((2, 2, NX, NY, 16, HALF), BF16), ((16, W), BF16), ((4, 16, KL), BF16), ((2, 16, 128), BF16), ((512, 128), F32), ((512, 128), F32), ((512, 128), F32),
+        ((512, wkv_b.shape[1]), BF16), ((2, 512, 128), BF16), ((512, 512), BF16), ((16, 512), BF16),
         ((2, 2, 4, 4, 112, 256), BF16), ((2, 2, 4, 4, 112, 256), BF16),
         ((2, 4, 4, 112, 256), BF16), ((2, 4, 4, 112, 256), BF16),
         ((2, 2, 4, 112, 256), BF16), ((2, 2, 4, 112, 256), BF16),
@@ -686,7 +764,7 @@
         ((16, 1024), F32), ((2, 16, 16, 256), BF16), ((16, 16, 256), BF16), ((16, 16, 256), BF16),
         ((8, 16, 256), BF16),
     ]
-    counts = (3, 8, 8, 8, 8, 18, 18, 1, 1, 16, 16, 16, 16, 38, 38, 1, 1, 36, 36, 16, 16, 1, 1, 16, 16, 8, 8)
+    counts = (3, 8, 8, 16, 16, 36, 36, 1, 1, 16, 16, 16, 16, 28, 28, 1, 1, 36, 36, 16, 16, 1, 1, 16, 16, 8, 8, 2, 2)
     return pl.pallas_call(
         whole_kernel,
         out_shape=(jax.ShapeDtypeStruct((224, 512), BF16), jax.ShapeDtypeStruct((16, 224), BF16)),

time: 91.4 us -> 92.2 us (level)
  no operation moved by 1% of the time
where the time goes in v4:
time: 92.2 us; the launch traced here: 92.1 us
  Pallas kernels  91.5 us (99%)
    pallas_call x1, Pallas kernels, whole(): pl.pallas_call(whole_kernel, out_shape=(jax.ShapeDtypeStruct((224, 512),...  89.8 us

profile of v4, /device:TPU:1, one launch (start us, length us, event | category | flops | bytes accessed | tf_op | source)
XLA Modules:
  0.0 92.1 jit_solution(1146011768808749663)
XLA Ops:
  0.6 89.8 %whole.1 = (bf16[224,512]{1,0:T(8,128)(2,1)}, bf16[16,224]{1,0:T(8,128)(2,1)}) custom-call(bf16[224,512]{1,0:T(8,128)(2,1)} %bitcast.2, bf16[16,224]{1,0:T(8,128)(2,1)} %xd_ref.1, bf16[224,1536]{1,0:T(8,128)(2,1)} %wqa_ref.1, bf16[224,576]{1,0:T(8,128)(2,1)} %wkva_ref.1, f32[1536]{0:T(1024)} %qg_ref.1, f32[512]{0:T(512)} %kvg_ref.1, ...), custom_call_target="tpu_custom_call" | custom-call | tf_op jit(solution)/shard_map/whole/pallas_call | solution.py:768
  90.5 1.6 %hand_over.1 = (bf16[224,512]{1,0:T(8,128)(2,1)}, bf16[16,224]{1,0:T(8,128)(2,1)}) custom-call(bf16[224,512]{1,0:T(8,128)(2,1)} %get-tuple-element.6.a_ref, bf16[16,224]{1,0:T(8,128)(2,1)} %get-tuple-element.7.b_ref), custom_call_target="tpu_custom_call" | custom-call | tf_op jit(solution)/shard_map/hand_over/pallas_call | solution.py:788

commit v5 on v4

--- a/solution.py
+++ b/solution.py
@@ -176,7 +176,7 @@
     rows_s, square_s, square_in, gain_s,
     zb, zd, qabs_s, qrope_s, pos_s, cos_s, sin_s, kv_s, turn_s, o_s, od_s,
     t0, t1, tc0, tc1, tnear0, tnear1, tfar0, tfar1, tq0, tq1, tqin0, tqin1,
-    dd, dt, dc, dn, dz,
+    dt, dc, dn, dz,
     ws, zs, zr, cs, cr, rs, rr, ds, dr, es, er, gs, gr, ks, kr, ms, mr,
     us, ur, vs, vr, fs, fr, hs, hr, ys, yr, qs, qr,
 ):
@@ -262,10 +262,12 @@
             k = next_of(pos_p, order[i])
             p[self.s, c, k] = p[self.s, c, k] + came[self.s, k]
 
-        def first(self):
+        def far(self):
             for h in range(2):
                 self.take(0, h)
                 self.rings[h].start_far()
+
+        def near(self):
             for h in range(2):
                 self.take(1, h)
                 self.take(2, h)
@@ -367,9 +369,9 @@
 
     lax.fori_loop(1, 8, send_z, 0)
     product(1)
+    f0.far()
+    f0.near()
     f1.swap()
-    f0.first()
-    f1.first()
 
     def wait_z(step, carry):
         zz, other, device = z_peer(step)
@@ -387,7 +389,9 @@
         dec[:, :, lo : lo + wide] = val.reshape(2, 8, wide)
     dec_core = remote(dec.at[1 - c], dec_in, ds.at[0], dr.at[0], peer)
     dec_core.start()
+    f1.far()
     f0.pass_on()
+    f1.near()
 
     q_gain, kv_gain = qg_ref[...].reshape(1, QL), kvg_ref[...].reshape(1, KL)
     gain_s[...] = jnp.zeros_like(gain_s)
@@ -427,7 +431,6 @@
 
     f0.second()
     f1.pass_on()
-    loads[0].wait()
 
     def turn_wo(k, carry):
         cut = pl.multiple_of(k * 896, 128)
@@ -453,6 +456,11 @@
     f1.second()
     f0.norm()
     f0.gather_one()
+
+    loads[0].wait()
+    lax.fori_loop(0, 3, turn_wo, 0)
+    f0.gather_two()
+    f1.rows()
 
     def wait_sum(step, carry):
         other, device = chip_peer(x, y, c, step)
@@ -465,8 +473,6 @@
     rows_in[c, :, QL + KL : W] = total[:, 128:]
     dec_mate = remote(rows_in.at[c], rows_in.at[c], ms.at[0], mr.at[0], peer)
     dec_mate.start()
-    f1.rows()
-    f0.gather_two()
     f1.norm()
     f1.gather_one()
     dec_mate.wait()
@@ -484,11 +490,13 @@
     for h in range(heads):
         up_k = wkvb[:, wide * h : wide * h + NOPE]
         qabs_s[h] = lax.dot_general(dec_nope[h], up_k, NT, preferred_element_type=F32).astype(BF16)
-        qrope_s[h // 2] = dec_rope[h // 2]
+        if h % 2:
+            qrope_s[h] = pltpu.roll(dec_rope[h // 2].astype(F32), 64, 1).astype(BF16)
+        else:
+            qrope_s[h] = dec_rope[h // 2]
+    lax.fori_loop(3, 8, turn_wo, 0)
+    f0.gather_mate()
     f1.gather_two()
-    lax.fori_loop(0, 4, turn_wo, 0)
-    f0.gather_mate()
-    lax.fori_loop(4, 8, turn_wo, 0)
     f0.gather_end()
 
     def project(s):
@@ -500,12 +508,11 @@
         turn_s[1, rows, :] = pltpu.roll(turn.astype(F32), 64, 1).astype(BF16)
 
     def block(s):
-        def attend(j, carry):
-            i = 2 * s + j
-            first = pl.multiple_of(i * 128, 128)
-            begin = pl.multiple_of(jnp.maximum(i - 1, 0) * 128, 128)
-            rows, keys = pl.ds(first, 128), pl.ds(begin, 256)
-            chips = pl.ds(2 * j, 2)
+        for j in range(2):
+            first = 256 * s + 128 * j
+            begin = max(first - 128, 0)
+            rows, keys = slice(first, first + 128), slice(begin, begin + 256)
+            chips = slice(2 * j, 2 * j + 2)
             query = jnp.dot(
                 zb[s, 0, chips, :, :, :cut_q].reshape(128, cut_q), wqb[:cut_q, :], preferred_element_type=F32
             )
@@ -517,60 +524,73 @@
             other = begin + lax.broadcasted_iota(jnp.int32, (128, 256), 1)
             back = (own - other).astype(F32)
             keep = (back >= 0) & (back <= jnp.concatenate([pos_s[rows, :]] * 2, axis=1))
+            scores = []
             for h in range(heads):
                 q = jnp.concatenate([nope[h], rope[h // 2]], axis=1)
                 k = jnp.concatenate([kv_s[keys, wide * h : wide * h + NOPE], turn_s[h % 2, keys, :]], axis=1)
-                s_h = lax.dot_general(q, k, NT, preferred_element_type=F32) * scale
-                s_h = jnp.where(keep, s_h, -1e30)
-                e = jnp.exp(s_h - jnp.max(s_h, axis=-1, keepdims=True))
-                p = (e * (1.0 / jnp.sum(e, axis=-1, keepdims=True))).astype(BF16)
+                scores.append(lax.dot_general(q, k, NT, preferred_element_type=F32))
+            scores = jnp.concatenate(scores, axis=0) * scale
+            scores = jnp.where(jnp.concatenate([keep] * heads, axis=0), scores, -1e30)
+            e = jnp.exp(scores - jnp.max(scores, axis=-1, keepdims=True))
+            p = (e * (1.0 / jnp.sum(e, axis=-1, keepdims=True))).astype(BF16)
+            for h in range(heads):
                 v = kv_s[keys, wide * h + NOPE : wide * h + wide]
-                o = jnp.dot(p, v, preferred_element_type=F32)
+                o = jnp.dot(p[128 * h : 128 * h + 128], v, preferred_element_type=F32)
                 o_s[rows, VD * h : VD * h + VD] = o.astype(BF16)
-            return carry
-
-        lax.fori_loop(0, 2, attend, 0)
 
     def decode():
         latent, own_lat = zb[:, 1, :, :, :, QL - cut_q : cut_q].reshape(512, KL), zd[:, QL : QL + KL]
-        turns, own_turn = (turn_s[0], turn_s[1]), zd[:, QL + KL : W].astype(F32)
-        own_turns = (own_turn.astype(BF16), pltpu.roll(own_turn, 64, 1).astype(BF16))
+        own_turn = zd[:, QL + KL : W]
         at = lax.broadcasted_iota(jnp.int32, (16, 512), 1).astype(F32)
         keep = (at < end_col) & (at >= end_col - len_col)
-        diag = i16 == j16
+        keep = jnp.concatenate([keep] * heads, axis=0)
+        diag = jnp.concatenate([i16 == j16] * heads, axis=0)
+        q_abs, q_rope = qabs_s[...].reshape(16 * heads, KL), qrope_s[...].reshape(16 * heads, 128)
+        s = lax.dot_general(q_abs, latent, NT, preferred_element_type=F32)
+        s = (s + lax.dot_general(q_rope, turn_s[0], NT, preferred_element_type=F32)) * scale
+        s = jnp.where(keep, s, -1e30)
+        t = lax.dot_general(q_abs, own_lat, NT, preferred_element_type=F32)
+        t = (t + lax.dot_general(q_rope, own_turn, NT, preferred_element_type=F32)) * scale
+        t = jnp.where(diag, t, -1e30)
+        top = jnp.maximum(jnp.max(s, axis=-1, keepdims=True), jnp.max(t, axis=-1, keepdims=True))
+        e, f = jnp.exp(s - top), jnp.exp(t - top)
+        part = 1.0 / (jnp.sum(e, axis=-1, keepdims=True) + jnp.sum(f, axis=-1, keepdims=True))
+        lat = jnp.dot((e * part).astype(BF16), latent, preferred_element_type=F32)
+        lat = (lat + jnp.dot((f * part).astype(BF16), own_lat, preferred_element_type=F32)).astype(BF16)
         for h in range(heads):
-            q_abs, q_rope = qabs_s[h], qrope_s[h // 2]
-            s = lax.dot_general(q_abs, latent, NT, preferred_element_type=F32)
-            s = (s + lax.dot_general(q_rope, turns[h % 2], NT, preferred_element_type=F32)) * scale
-            s = jnp.where(keep, s, -1e30)
-            t = lax.dot_general(q_abs, own_lat, NT, preferred_element_type=F32)
-            t = (t + lax.dot_general(q_rope, own_turns[h % 2], NT, preferred_element_type=F32)) * scale
-            t = jnp.where(diag, t, -1e30)
-            top = jnp.maximum(jnp.max(s, axis=-1, keepdims=True), jnp.max(t, axis=-1, keepdims=True))
-            e, f = jnp.exp(s - top), jnp.exp(t - top)
-            part = 1.0 / (jnp.sum(e, axis=-1, keepdims=True) + jnp.sum(f, axis=-1, keepdims=True))
-            lat = jnp.dot((e * part).astype(BF16), latent, preferred_element_type=F32)
-            lat = lat + jnp.dot((f * part).astype(BF16), own_lat, preferred_element_type=F32)
             up_v = wkvb[:, wide * h + NOPE : wide * h + wide]
-            o = jnp.dot(lat.astype(BF16), up_v, preferred_element_type=F32)
+            o = jnp.dot(lat[16 * h : 16 * h + 16], up_v, preferred_element_type=F32)
             od_s[:, VD * h : VD * h + VD] = o.astype(BF16)
+
+    def decode_out():
+        for k in range(8):
+            val = jnp.dot(od_s[...], wo[:, 896 * k : 896 * k + 896], preferred_element_type=F32)
+            for j in range(4):
+                at = 224 * j // 128 * 128
+                if at + 384 <= 896:
+                    v = val[:, at : at + 384]
+                else:
+                    v = jnp.concatenate([val[:, at:896], val[:, : at + 384 - 896]], axis=1)
+                if 224 * j - at:
+                    v = pltpu.roll(v, 384 - (224 * j - at), 1)
+                dt[j % 2, 2 * k + j // 2] = v[:, :256].astype(BF16)
 
     def output(s):
         far_x, far_y = next_of(x, 2), next_of(y, 2) // 2
 
-        def part(n, carry):
-            k = jnp.where(
-                n < 2,
-                2 * far_x + n,
-                jnp.where(n < 5, 2 * next_of(far_x, n - 1) + far_y, 2 * next_of(far_x, n - 4) + 1 - far_y),
-            )
+        def part(n):
+            if n < 2:
+                k = 2 * far_x + n
+            elif n < 5:
+                k = 2 * next_of(far_x, n - 1) + far_y
+            else:
+                k = 2 * next_of(far_x, n - 4) + 1 - far_y
             xx, yy = k // 2, 2 * lax.rem(k, 2)
             w = wot[pl.ds(pl.multiple_of(k * 896, 128), 896), :]
             val = lax.dot_general(w, o_s[256 * s : 256 * s + 256, :], NT, preferred_element_type=F32).astype(BF16)
             for j in range(4):
                 t0[s, j % 2, xx, yy + j // 2] = val[224 * j : 224 * j + 112]
                 t1[s, j % 2, yy + j // 2, xx] = val[224 * j + 112 : 224 * j + 224]
-            return carry
 
         return part
 
@@ -653,9 +673,11 @@
 
     def produce(stage):
         part = output(stage.s)
-        lax.fori_loop(0, 5, part, 0)
+        for n in range(5):
+            part(n)
         stage.swap((0,))
-        lax.fori_loop(5, 8, part, 0)
+        for n in range(5, 8):
+            part(n)
         stage.swap((1, 2, 3))
 
     project(0)
@@ -666,30 +688,13 @@
     f1.gather_end()
     project(1)
     block(1)
+    decode()
+    decode_out()
+    dec_swap = remote(dt.at[1 - c], dc, fs.at[0], fr.at[0], peer)
+    dec_swap.start()
     s0.pass_on()
     produce(s1)
     s1.first()
-    s0.second()
-    decode()
-
-    dd[...] = jnp.zeros_like(dd)
-
-    def dec_part(k, carry):
-        w = wo[:, pl.ds(pl.multiple_of(k * 896, 128), 896)]
-        dd[:, :896] = jnp.dot(od_s[...], w, preferred_element_type=F32)
-        for j in range(4):
-            at = 224 * j // 128 * 128
-            v = dd[:, at : at + 384]
-            if 224 * j - at:
-                v = pltpu.roll(v, 384 - (224 * j - at), 1)
-            dt[j % 2, 2 * k + j // 2] = v[:, :256].astype(BF16)
-        return carry
-
-    lax.fori_loop(0, 8, dec_part, 0)
-    dec_swap = remote(dt.at[1 - c], dc, fs.at[0], fr.at[0], peer)
-    dec_swap.start()
-    s1.pass_on()
-    s0.finish()
     dec_swap.wait()
     dt[c] = (dt[c].astype(F32) + dc[...].astype(F32)).astype(BF16)
 
@@ -700,6 +705,7 @@
 
     lax.fori_loop(1, 16, send_out, 0)
     dn[chip] = dt[c, chip]
+    s0.second()
 
     def wait_out(step, carry):
         other, device = chip_peer(x, y, c, step)
@@ -715,7 +721,8 @@
         return carry
 
     lax.fori_loop(1, 8, send_back, 0)
-    s1.second()
+    s1.pass_on()
+    s0.finish()
 
     def wait_back(step, carry):
         zz, _, device = z_peer(step)
@@ -727,7 +734,7 @@
     sel_out = jnp.where(jj.astype(F32) == wanted, 1.0, 0.0).astype(BF16)
     picked = jnp.dot(sel_out, dz[...].reshape(128, 256), preferred_element_type=F32)
     outd_ref[...] = picked[:, :224].astype(BF16)
-
+    s1.second()
     s1.finish()
     for copy in copies:
         copy.wait_send()
@@ -753,7 +760,7 @@
         ((8,) + xd.shape, BF16), ((2, 8, W), F32), ((8, W), F32),
         ((16, 8, 256), F32), ((16, 8, 256), F32), ((16, 8, 128), F32), ((2, 8, W), F32),
         ((2, 16, HALF), F32), ((2, 2, 16, 128), F32), ((2, 16, 128), F32), ((8, HALF), F32),
-        ((2, 2, NX, NY, 16, HALF), BF16), ((16, W), BF16), ((4, 16, KL), BF16), ((2, 16, 128), BF16), ((512, 128), F32), ((512, 128), F32), ((512, 128), F32),
+        ((2, 2, NX, NY, 16, HALF), BF16), ((16, W), BF16), ((4, 16, KL), BF16), ((4, 16, 128), BF16), ((512, 128), F32), ((512, 128), F32), ((512, 128), F32),
         ((512, wkv_b.shape[1]), BF16), ((2, 512, 128), BF16), ((512, 512), BF16), ((16, 512), BF16),
         ((2, 2, 4, 4, 112, 256), BF16), ((2, 2, 4, 4, 112, 256), BF16),
         ((2, 4, 4, 112, 256), BF16), ((2, 4, 4, 112, 256), BF16),
@@ -761,7 +768,7 @@
         ((2, 4, 112, 256), BF16), ((2, 4, 112, 256), BF16),
         ((2, 4, 112, 256), BF16), ((2, 4, 112, 256), BF16),
         ((2, 3, 112, 256), BF16), ((2, 3, 112, 256), BF16),
-        ((16, 1024), F32), ((2, 16, 16, 256), BF16), ((16, 16, 256), BF16), ((16, 16, 256), BF16),
+        ((2, 16, 16, 256), BF16), ((16, 16, 256), BF16), ((16, 16, 256), BF16),
         ((8, 16, 256), BF16),
     ]
     counts = (3, 8, 8, 16, 16, 36, 36, 1, 1, 16, 16, 16, 16, 28, 28, 1, 1, 36, 36, 16, 16, 1, 1, 16, 16, 8, 8, 2, 2)

time: 92.2 us -> 85.9 us (0.932)
  the two profiles are of different devices: /device:TPU:1 before, /device:TPU:32 now
where the time goes in v5:
time: 85.9 us; the launch traced here: 85.8 us
  Pallas kernels  85.2 us (99%)
    pallas_call x1, Pallas kernels, whole(): pl.pallas_call(whole_kernel, out_shape=(jax.ShapeDtypeStruct((224, 512),...  83.5 us

profile of v5, /device:TPU:32, one launch (start us, length us, event | category | flops | bytes accessed | tf_op | source)
XLA Modules:
  0.0 85.8 jit_solution(8591335664044462640)
XLA Ops:
  0.6 83.5 %whole.1 = (bf16[224,512]{1,0:T(8,128)(2,1)}, bf16[16,224]{1,0:T(8,128)(2,1)}) custom-call(bf16[224,512]{1,0:T(8,128)(2,1)} %bitcast.2, bf16[16,224]{1,0:T(8,128)(2,1)} %xd_ref.1, bf16[224,1536]{1,0:T(8,128)(2,1)} %wqa_ref.1, bf16[224,576]{1,0:T(8,128)(2,1)} %wkva_ref.1, f32[1536]{0:T(1024)} %qg_ref.1, f32[512]{0:T(512)} %kvg_ref.1, ...), custom_call_target="tpu_custom_call" | custom-call | tf_op jit(solution)/shard_map/whole/pallas_call | solution.py:775
  84.2 1.6 %hand_over.1 = (bf16[224,512]{1,0:T(8,128)(2,1)}, bf16[16,224]{1,0:T(8,128)(2,1)}) custom-call(bf16[224,512]{1,0:T(8,128)(2,1)} %get-tuple-element.6.a_ref, bf16[16,224]{1,0:T(8,128)(2,1)} %get-tuple-element.7.b_ref), custom_call_target="tpu_custom_call" | custom-call | tf_op jit(solution)/shard_map/hand_over/pallas_call | solution.py:795

commit v6 on v5

--- a/solution.py
+++ b/solution.py
@@ -169,8 +169,8 @@
 
 
 def whole_kernel(
-    xt_ref, xd_ref, wqa_ref, wkva_ref, qg_ref, kvg_ref, freq_ref, len_ref, docs_ref, wqb_hbm, wkvb_hbm, wo_hbm,
-    out_ref, outd_ref,
+    xt_hbm, xd_ref, wqa_hbm, wkva_hbm, qg_ref, kvg_ref, freq_ref, len_ref, docs_ref, wqb_hbm, wkvb_hbm, wo_hbm,
+    out_ref, outd_ref, xt_ref, wqa_ref, wkva_ref,
     wqb, wkvb, wo, wot, wkv_s, p0, p1, c0, c1, near0, near1, far0, far1, q0, q1, in0, in1,
     xd_all, dec, dec_in, tiles, tiles_in, sums_in, rows_in,
     rows_s, square_s, square_in, gain_s,
@@ -189,10 +189,17 @@
     greet_start(x, y, c)
     loads = [
         pltpu.make_async_copy(src, dst, ws.at[i])
-        for i, (src, dst) in enumerate(((wo_hbm, wo), (wkvb_hbm, wkvb), (wqb_hbm, wqb)))
+        for i, (src, dst) in enumerate(
+            (
+                (wo_hbm, wo), (wkvb_hbm, wkvb), (wqb_hbm, wqb),
+                (xt_hbm, xt_ref), (wqa_hbm, wqa_ref), (wkva_hbm, wkva_ref),
+            )
+        )
     ]
-    for load in loads:
+    for load in loads[3:]:
         load.start()
+    for load in loads[3:]:
+        load.wait()
 
     wkv_s[...] = jnp.zeros_like(wkv_s)
     wkv_s[:, : KL + RD] = wkva_ref[...]
@@ -372,12 +379,15 @@
     f0.far()
     f0.near()
     f1.swap()
+    for load in loads[1:3]:
+        load.start()
 
     def wait_z(step, carry):
         zz, other, device = z_peer(step)
         remote(xd_ref, xd_all.at[zz], zs.at[step], zr.at[step], device).wait()
         return carry
 
+    f1.far()
     lax.fori_loop(1, 8, wait_z, 0)
     ii = lax.broadcasted_iota(jnp.int32, (16, 128), 0)
     jj = lax.broadcasted_iota(jnp.int32, (16, 128), 1)
@@ -389,9 +399,9 @@
         dec[:, :, lo : lo + wide] = val.reshape(2, 8, wide)
     dec_core = remote(dec.at[1 - c], dec_in, ds.at[0], dr.at[0], peer)
     dec_core.start()
-    f1.far()
     f0.pass_on()
     f1.near()
+    loads[0].start()
 
     q_gain, kv_gain = qg_ref[...].reshape(1, QL), kvg_ref[...].reshape(1, KL)
     gain_s[...] = jnp.zeros_like(gain_s)
@@ -415,6 +425,7 @@
         cos_s[part, :], sin_s[part, :] = turn_tables(pos_s[part, :], freq)
     cosd, sind = turn_tables(jnp.broadcast_to(len_col, (16, 128)), freq)
 
+    f0.second()
     dec_core.wait()
     mine = dec[c] + dec_in[...]
     for j in range(16):
@@ -429,7 +440,6 @@
     lax.fori_loop(1, 16, send_tile, 0)
     tiles_in[chip] = tiles[chip]
 
-    f0.second()
     f1.pass_on()
 
     def turn_wo(k, carry):
@@ -437,31 +447,36 @@
         wot[pl.ds(cut, 896), :] = wo[:, pl.ds(cut, 896)].T
         return carry
 
-    def wait_tile(step, carry):
-        other, device = chip_peer(x, y, c, step)
-        remote(tiles.at[other], tiles_in.at[chip], es.at[step], er.at[step], device).wait()
-        return carry
-
-    lax.fori_loop(1, 16, wait_tile, 0)
-    total = jnp.sum(tiles_in[...], axis=0)
-    sums_in[chip] = total[:, :128]
-
-    def send_sum(step, carry):
-        other, device = chip_peer(x, y, c, step)
-        remote(sums_in.at[chip], sums_in.at[chip], gs.at[step], gr.at[step], device).start()
-        return carry
-
-    lax.fori_loop(1, 16, send_sum, 0)
     f0.rows()
-    f1.second()
     f0.norm()
     f0.gather_one()
+    f1.second()
 
     loads[0].wait()
     lax.fori_loop(0, 3, turn_wo, 0)
     f0.gather_two()
     f1.rows()
 
+    f1.norm()
+    f1.gather_one()
+    def wait_tile(step, carry):
+        other, device = chip_peer(x, y, c, step)
+        remote(tiles.at[other], tiles_in.at[chip], es.at[step], er.at[step], device).wait()
+        return carry
+
+    lax.fori_loop(1, 16, wait_tile, 0)
+    total = jnp.sum(tiles_in[...], axis=0)
+    sums_in[chip] = total[:, :128]
+
+    def send_sum(step, carry):
+        other, device = chip_peer(x, y, c, step)
+        remote(sums_in.at[chip], sums_in.at[chip], gs.at[step], gr.at[step], device).start()
+        return carry
+
+    lax.fori_loop(1, 16, send_sum, 0)
+    lax.fori_loop(3, 5, turn_wo, 0)
+    f1.gather_two()
+    f0.gather_mate()
     def wait_sum(step, carry):
         other, device = chip_peer(x, y, c, step)
         remote(sums_in.at[chip], sums_in.at[chip], gs.at[step], gr.at[step], device).wait()
@@ -473,30 +488,12 @@
     rows_in[c, :, QL + KL : W] = total[:, 128:]
     dec_mate = remote(rows_in.at[c], rows_in.at[c], ms.at[0], mr.at[0], peer)
     dec_mate.start()
-    f1.norm()
-    f1.gather_one()
-    dec_mate.wait()
-    q, kv, turn = latent_rows(rows_in[...].reshape(16, W), q_gain, kv_gain, cosd, sind)
-    zd[:, 0:QL] = q.astype(BF16)
-    zd[:, QL : QL + KL] = kv.astype(BF16)
-    zd[:, QL + KL : W] = turn.astype(BF16)
     heads = 4
     scale = 1.0 / float(NOPE + RD) ** 0.5
     wide = NOPE + VD
-    for load in loads[1:]:
+    for load in loads[1:3]:
         load.wait()
-    query = jnp.dot(zd[:, :QL], wqb[...], preferred_element_type=F32)
-    dec_nope, dec_rope = split_query(query, cosd, sind)
-    for h in range(heads):
-        up_k = wkvb[:, wide * h : wide * h + NOPE]
-        qabs_s[h] = lax.dot_general(dec_nope[h], up_k, NT, preferred_element_type=F32).astype(BF16)
-        if h % 2:
-            qrope_s[h] = pltpu.roll(dec_rope[h // 2].astype(F32), 64, 1).astype(BF16)
-        else:
-            qrope_s[h] = dec_rope[h // 2]
-    lax.fori_loop(3, 8, turn_wo, 0)
-    f0.gather_mate()
-    f1.gather_two()
+    lax.fori_loop(5, 8, turn_wo, 0)
     f0.gather_end()
 
     def project(s):
@@ -682,19 +679,34 @@
 
     project(0)
     block(0)
+    produce(s0)
     f1.gather_mate()
-    produce(s0)
     s0.first()
     f1.gather_end()
     project(1)
     block(1)
+    produce(s1)
+    s0.pass_on()
+    s1.first()
+    dec_mate.wait()
+    q, kv, turn = latent_rows(rows_in[...].reshape(16, W), q_gain, kv_gain, cosd, sind)
+    zd[:, 0:QL] = q.astype(BF16)
+    zd[:, QL : QL + KL] = kv.astype(BF16)
+    zd[:, QL + KL : W] = turn.astype(BF16)
+    query = jnp.dot(zd[:, :QL], wqb[...], preferred_element_type=F32)
+    dec_nope, dec_rope = split_query(query, cosd, sind)
+    for h in range(heads):
+        up_k = wkvb[:, wide * h : wide * h + NOPE]
+        qabs_s[h] = lax.dot_general(dec_nope[h], up_k, NT, preferred_element_type=F32).astype(BF16)
+        if h % 2:
+            qrope_s[h] = pltpu.roll(dec_rope[h // 2].astype(F32), 64, 1).astype(BF16)
+        else:
+            qrope_s[h] = dec_rope[h // 2]
     decode()
     decode_out()
     dec_swap = remote(dt.at[1 - c], dc, fs.at[0], fr.at[0], peer)
     dec_swap.start()
-    s0.pass_on()
-    produce(s1)
-    s1.first()
+    s0.second()
     dec_swap.wait()
     dt[c] = (dt[c].astype(F32) + dc[...].astype(F32)).astype(BF16)
 
@@ -705,7 +717,8 @@
 
     lax.fori_loop(1, 16, send_out, 0)
     dn[chip] = dt[c, chip]
-    s0.second()
+    s1.pass_on()
+    s0.finish()
 
     def wait_out(step, carry):
         other, device = chip_peer(x, y, c, step)
@@ -721,8 +734,7 @@
         return carry
 
     lax.fori_loop(1, 8, send_back, 0)
-    s1.pass_on()
-    s0.finish()
+    s1.second()
 
     def wait_back(step, carry):
         zz, _, device = z_peer(step)
@@ -734,7 +746,6 @@
     sel_out = jnp.where(jj.astype(F32) == wanted, 1.0, 0.0).astype(BF16)
     picked = jnp.dot(sel_out, dz[...].reshape(128, 256), preferred_element_type=F32)
     outd_ref[...] = picked[:, :224].astype(BF16)
-    s1.second()
     s1.finish()
     for copy in copies:
         copy.wait_send()
@@ -749,6 +760,7 @@
     hbm = pl.BlockSpec(memory_space=pl.ANY)
     dma = pltpu.SemaphoreType.DMA
     shapes = [
+        (xt.shape, BF16), (wq_a.shape, BF16), (wkv_a.shape, BF16),
         (wq_b.shape, BF16), (wkv_b.shape, BF16), (wo.shape, BF16), (wo.shape[::-1], BF16),
         ((wq_a.shape[0], W - QL), BF16),
         ((2, 2, 4, 4, 8, HALF), F32), ((2, 2, 4, 4, 8, HALF), F32),
@@ -771,11 +783,11 @@
         ((2, 16, 16, 256), BF16), ((16, 16, 256), BF16), ((16, 16, 256), BF16),
         ((8, 16, 256), BF16),
     ]
-    counts = (3, 8, 8, 16, 16, 36, 36, 1, 1, 16, 16, 16, 16, 28, 28, 1, 1, 36, 36, 16, 16, 1, 1, 16, 16, 8, 8, 2, 2)
+    counts = (6, 8, 8, 16, 16, 36, 36, 1, 1, 16, 16, 16, 16, 28, 28, 1, 1, 36, 36, 16, 16, 1, 1, 16, 16, 8, 8, 2, 2)
     return pl.pallas_call(
         whole_kernel,
         out_shape=(jax.ShapeDtypeStruct((224, 512), BF16), jax.ShapeDtypeStruct((16, 224), BF16)),
-        in_specs=[vm] * 9 + [hbm] * 3,
+        in_specs=[hbm, vm, hbm, hbm] + [vm] * 5 + [hbm] * 3,
         out_specs=(vm, vm),
         scratch_shapes=[pltpu.VMEM(shape, kind) for shape, kind in shapes] + [dma((n,)) for n in counts],
         compiler_params=pltpu.CompilerParams(

time: 85.9 us -> 82.1 us (0.956)
  the two profiles are of different devices: /device:TPU:32 before, /device:TPU:1 now
where the time goes in v6:
time: 82.1 us; the launch traced here: 82 us
  Pallas kernels  81.3 us (99%)
    pallas_call x1, Pallas kernels, whole(): pl.pallas_call(whole_kernel, out_shape=(jax.ShapeDtypeStruct((224, 512),...  79.7 us
    pallas_call x1, Pallas kernels, hand_over(): pl.pallas_call(hand_over_kernel, out_shape=(jax.ShapeDtypeStruct(a.shape,...  1.65 us

profile of v6, /device:TPU:1, one launch (start us, length us, event | category | flops | bytes accessed | tf_op | source)
XLA Modules:
  0.0 82.0 jit_solution(15442466772737902059)
XLA Ops:
  0.6 79.7 %whole.1 = (bf16[224,512]{1,0:T(8,128)(2,1)}, bf16[16,224]{1,0:T(8,128)(2,1)}) custom-call(bf16[224,512]{1,0:T(8,128)(2,1)} %bitcast.2, bf16[16,224]{1,0:T(8,128)(2,1)} %xd_ref.1, bf16[224,1536]{1,0:T(8,128)(2,1)} %wqa_hbm.1, bf16[224,576]{1,0:T(8,128)(2,1)} %wkva_hbm.1, f32[1536]{0:T(1024)} %qg_ref.1, f32[512]{0:T(512)} %kvg_ref.1, ...), custom_call_target="tpu_custom_call" | custom-call | tf_op jit(solution)/shard_map/whole/pallas_call | solution.py:787
  80.3 1.6 %hand_over.1 = (bf16[224,512]{1,0:T(8,128)(2,1)}, bf16[16,224]{1,0:T(8,128)(2,1)}) custom-call(bf16[224,512]{1,0:T(8,128)(2,1)} %get-tuple-element.6.a_ref, bf16[16,224]{1,0:T(8,128)(2,1)} %get-tuple-element.7.b_ref), custom_call_target="tpu_custom_call" | custom-call | tf_op jit(solution)/shard_map/hand_over/pallas_call | solution.py:807

commit v7 on v6

--- a/solution.py
+++ b/solution.py
@@ -169,8 +169,8 @@
 
 
 def whole_kernel(
-    xt_hbm, xd_ref, wqa_hbm, wkva_hbm, qg_ref, kvg_ref, freq_ref, len_ref, docs_ref, wqb_hbm, wkvb_hbm, wo_hbm,
-    out_ref, outd_ref, xt_ref, wqa_ref, wkva_ref,
+    xt_hbm, xd_hbm, wqa_hbm, wkva_hbm, qg_hbm, kvg_hbm, freq_hbm, len_hbm, docs_hbm, wqb_hbm, wkvb_hbm, wo_hbm,
+    out_ref, outd_ref, xt_ref, wqa_ref, wkva_ref, xd_ref, qg_ref, kvg_ref, freq_ref, len_ref, docs_ref,
     wqb, wkvb, wo, wot, wkv_s, p0, p1, c0, c1, near0, near1, far0, far1, q0, q1, in0, in1,
     xd_all, dec, dec_in, tiles, tiles_in, sums_in, rows_in,
     rows_s, square_s, square_in, gain_s,
@@ -186,19 +186,20 @@
     peer = {"tp": tp_of(x, y, 1 - c)}
     xp, xm = {"tp": tp_of(next_of(x, 1), y, c)}, {"tp": tp_of(next_of(x, -1), y, c)}
     yp, ym = {"tp": tp_of(x, next_of(y, 1), c)}, {"tp": tp_of(x, next_of(y, -1), c)}
-    greet_start(x, y, c)
     loads = [
         pltpu.make_async_copy(src, dst, ws.at[i])
         for i, (src, dst) in enumerate(
             (
                 (wo_hbm, wo), (wkvb_hbm, wkvb), (wqb_hbm, wqb),
-                (xt_hbm, xt_ref), (wqa_hbm, wqa_ref), (wkva_hbm, wkva_ref),
+                (xt_hbm, xt_ref), (wqa_hbm, wqa_ref), (wkva_hbm, wkva_ref), (xd_hbm, xd_ref), (qg_hbm, qg_ref),
+                (kvg_hbm, kvg_ref), (freq_hbm, freq_ref), (len_hbm, len_ref), (docs_hbm, docs_ref),
             )
         )
     ]
     for load in loads[3:]:
         load.start()
-    for load in loads[3:]:
+    greet_start(x, y, c)
+    for load in loads[3:6]:
         load.wait()
 
     wkv_s[...] = jnp.zeros_like(wkv_s)
@@ -367,6 +368,8 @@
     product(0)
     greet_wait()
     f0.swap()
+    for load in loads[6:]:
+        load.wait()
     xd_all[z] = xd_ref[...]
 
     def send_z(step, carry):
@@ -638,11 +641,10 @@
                 ring.pass_on()
 
         def second(self):
-            for side in range(2):
-                tq0[self.s, :, :, half[side]] = self.rings[0].result(side).astype(BF16)
-                tq1[self.s, :, :, half[side]] = self.rings[1].result(side).astype(BF16)
-            for d in (2, 1, 3):
-                for h, (data, box, pos_q, dev) in enumerate(self.lasts):
+            for h, (data, box, pos_q, dev) in enumerate(self.lasts):
+                for side in range(2):
+                    data[self.s, :, :, half[side]] = self.rings[h].result(side).astype(BF16)
+                for d in (2, 1, 3):
                     n = 18 * self.s + 12 + 3 * h + d - 1
                     copy = remote(
                         data.at[self.s, next_of(pos_q, d)], box.at[self.s, d - 1], us.at[n], ur.at[n], {"tp": dev(d)}
@@ -760,7 +762,8 @@
     hbm = pl.BlockSpec(memory_space=pl.ANY)
     dma = pltpu.SemaphoreType.DMA
     shapes = [
-        (xt.shape, BF16), (wq_a.shape, BF16), (wkv_a.shape, BF16),
+        (xt.shape, BF16), (wq_a.shape, BF16), (wkv_a.shape, BF16), (xd.shape, BF16), (q_gain.shape, F32),
+        (kv_gain.shape, F32), (freq.shape, F32), (doc_len.shape, jnp.int32), (docs.shape, jnp.int32),
         (wq_b.shape, BF16), (wkv_b.shape, BF16), (wo.shape, BF16), (wo.shape[::-1], BF16),
         ((wq_a.shape[0], W - QL), BF16),
         ((2, 2, 4, 4, 8, HALF), F32), ((2, 2, 4, 4, 8, HALF), F32),
@@ -783,11 +786,11 @@
         ((2, 16, 16, 256), BF16), ((16, 16, 256), BF16), ((16, 16, 256), BF16),
         ((8, 16, 256), BF16),
     ]
-    counts = (6, 8, 8, 16, 16, 36, 36, 1, 1, 16, 16, 16, 16, 28, 28, 1, 1, 36, 36, 16, 16, 1, 1, 16, 16, 8, 8, 2, 2)
+    counts = (12, 8, 8, 16, 16, 36, 36, 1, 1, 16, 16, 16, 16, 28, 28, 1, 1, 36, 36, 16, 16, 1, 1, 16, 16, 8, 8, 2, 2)
     return pl.pallas_call(
         whole_kernel,
         out_shape=(jax.ShapeDtypeStruct((224, 512), BF16), jax.ShapeDtypeStruct((16, 224), BF16)),
-        in_specs=[hbm, vm, hbm, hbm] + [vm] * 5 + [hbm] * 3,
+        in_specs=[hbm] * 12,
         out_specs=(vm, vm),
         scratch_shapes=[pltpu.VMEM(shape, kind) for shape, kind in shapes] + [dma((n,)) for n in counts],
         compiler_params=pltpu.CompilerParams(

time: 82.1 us -> 82 us (level)
  no operation moved by 1% of the time
where the time goes in v7:
time: 82 us; the launch traced here: 81.9 us
  Pallas kernels  81.3 us (99%)
    pallas_call x1, Pallas kernels, whole(): pl.pallas_call(whole_kernel, out_shape=(jax.ShapeDtypeStruct((224, 512),...  79.6 us
    pallas_call x1, Pallas kernels, hand_over(): pl.pallas_call(hand_over_kernel, out_shape=(jax.ShapeDtypeStruct(a.shape,...  1.65 us

profile of v7, /device:TPU:1, one launch (start us, length us, event | category | flops | bytes accessed | tf_op | source)
XLA Modules:
  0.0 81.9 jit_solution(12691441218057550741)
XLA Ops:
  0.6 79.6 %whole.1 = (bf16[224,512]{1,0:T(8,128)(2,1)}, bf16[16,224]{1,0:T(8,128)(2,1)}) custom-call(bf16[224,512]{1,0:T(8,128)(2,1)} %bitcast.2, bf16[16,224]{1,0:T(8,128)(2,1)} %xd_hbm.1, bf16[224,1536]{1,0:T(8,128)(2,1)} %wqa_hbm.1, bf16[224,576]{1,0:T(8,128)(2,1)} %wkva_hbm.1, f32[1536]{0:T(1024)} %qg_hbm.1, f32[512]{0:T(512)} %kvg_hbm.1, ...), custom_call_target="tpu_custom_call" | custom-call | tf_op jit(solution)/shard_map/whole/pallas_call | solution.py:790
  80.3 1.6 %hand_over.1 = (bf16[224,512]{1,0:T(8,128)(2,1)}, bf16[16,224]{1,0:T(8,128)(2,1)}) custom-call(bf16[224,512]{1,0:T(8,128)(2,1)} %get-tuple-element.6.a_ref, bf16[16,224]{1,0:T(8,128)(2,1)} %get-tuple-element.7.b_ref), custom_call_target="tpu_custom_call" | custom-call | tf_op jit(solution)/shard_map/hand_over/pallas_call | solution.py:810

commit v8 on v7

--- a/solution.py
+++ b/solution.py
@@ -721,6 +721,7 @@
     dn[chip] = dt[c, chip]
     s1.pass_on()
     s0.finish()
+    s1.second()
 
     def wait_out(step, carry):
         other, device = chip_peer(x, y, c, step)
@@ -736,7 +737,6 @@
         return carry
 
     lax.fori_loop(1, 8, send_back, 0)
-    s1.second()
 
     def wait_back(step, carry):
         zz, _, device = z_peer(step)

time: 82 us -> 82 us (level)
  no operation moved by 1% of the time
where the time goes in v8:
time: 82 us; the launch traced here: 81.9 us
  Pallas kernels  81.3 us (99%)
    pallas_call x1, Pallas kernels, whole(): pl.pallas_call(whole_kernel, out_shape=(jax.ShapeDtypeStruct((224, 512),...  79.6 us
    pallas_call x1, Pallas kernels, hand_over(): pl.pallas_call(hand_over_kernel, out_shape=(jax.ShapeDtypeStruct(a.shape,...  1.65 us

profile of v8, /device:TPU:1, one launch (start us, length us, event | category | flops | bytes accessed | tf_op | source)
XLA Modules:
  0.0 81.9 jit_solution(3704736876011496714)
XLA Ops:
  0.6 79.6 %whole.1 = (bf16[224,512]{1,0:T(8,128)(2,1)}, bf16[16,224]{1,0:T(8,128)(2,1)}) custom-call(bf16[224,512]{1,0:T(8,128)(2,1)} %bitcast.2, bf16[16,224]{1,0:T(8,128)(2,1)} %xd_hbm.1, bf16[224,1536]{1,0:T(8,128)(2,1)} %wqa_hbm.1, bf16[224,576]{1,0:T(8,128)(2,1)} %wkva_hbm.1, f32[1536]{0:T(1024)} %qg_hbm.1, f32[512]{0:T(512)} %kvg_hbm.1, ...), custom_call_target="tpu_custom_call" | custom-call | tf_op jit(solution)/shard_map/whole/pallas_call | solution.py:790
  80.3 1.6 %hand_over.1 = (bf16[224,512]{1,0:T(8,128)(2,1)}, bf16[16,224]{1,0:T(8,128)(2,1)}) custom-call(bf16[224,512]{1,0:T(8,128)(2,1)} %get-tuple-element.6.a_ref, bf16[16,224]{1,0:T(8,128)(2,1)} %get-tuple-element.7.b_ref), custom_call_target="tpu_custom_call" | custom-call | tf_op jit(solution)/shard_map/hand_over/pallas_call | solution.py:810
